TPU v7x, 32 devices: a whole 2x2x4 slice. The times are simulated.
32 devices in a mesh: wide: 16 (over z, y, core), narrow: 2 (over x).
Axes of the slice: x: 2, y: 2, z: 4, core: 2. Of those that a mesh axis runs over, the one named last changes fastest.
Arguments:
- key_grads: bfloat16 [16, 2, 2, 2048, 512], P('wide', 'narrow'), may hold values from -1600 to 1600
- router_grads: bfloat16 [16, 2, 2, 64, 2048], P('wide', 'narrow'), may hold values from -1600 to 1600
- gain_grads: bfloat16 [16, 2, 2, 2048], P('wide', 'narrow'), may hold values from -1600 to 1600
- key_master: float32 [2048, 512], P('narrow'), may hold values from -3 to 3
- key_first: float32 [2048, 512], P('narrow'), may hold values from -3 to 3
- key_second: float32 [2048, 512], P('narrow'), may hold values from 0.01 to 1
- router_master: float32 [64, 2048], P(None, 'narrow'), may hold values from -3 to 3
- router_first: float32 [64, 2048], P(None, 'narrow'), may hold values from -3 to 3
- router_second: float32 [64, 2048], P(None, 'narrow'), may hold values from 0.01 to 1
- gain_master: float32 [2048], P('narrow'), may hold values from 0.5 to 1.5
- gain_first: float32 [2048], P('narrow'), may hold values from -3 to 3
- gain_second: float32 [2048], P('narrow'), may hold values from 0.01 to 1
Outputs:
- key_master_new: float32 [2048, 512], P('narrow')
- key_first_new: float32 [2048, 512], P('narrow')
- key_second_new: float32 [2048, 512], P('narrow')
- router_master_new: float32 [64, 2048], P(None, 'narrow')
- router_first_new: float32 [64, 2048], P(None, 'narrow')
- router_second_new: float32 [64, 2048], P(None, 'narrow')
- gain_master_new: float32 [2048], P('narrow')
- gain_first_new: float32 [2048], P('narrow')
- gain_second_new: float32 [2048], P('narrow')
- key_weight: bfloat16 [2048, 512], replicated
- router_weight: bfloat16 [64, 2048], replicated
- gain_weight: bfloat16 [2048], replicated
All inputs are finite; a program needn't handle non-finite values.
Results may differ from a plain program's by a relative error of at most 0.002.
Values may be sent and summed in bfloat16 or wider, within the bound.
A program may use at most 64 MiB of HBM per device.

v0:
```python
import math

import jax
import jax.numpy as jnp
from jax import lax
from jax.sharding import PartitionSpec as P

D = 2048
KEY_WIDTH = 512
EXPERTS = 64


beta_one = 0.9
beta_two = 0.95
step_rate = 0.01
epsilon = 1e-08
bias_one = 1.0 - 0.9**10
bias_two = 1.0 - 0.95**10


def micro_total(grad_stack):
    summed = jnp.sum(grad_stack[0, 0].astype(jnp.float32), axis=0)
    rounded = lax.optimization_barrier(summed.astype(jnp.bfloat16))
    return rounded.astype(jnp.float32)


def adamw(master, first_moment, second, gradient, factor, decay_rate):
    scaled = factor * gradient
    first_new = beta_one * first_moment + (1.0 - beta_one) * scaled
    second_new = beta_two * second + (1.0 - beta_two) * scaled * scaled
    update = (
        first_new / bias_one / (jnp.sqrt(second_new / bias_two) + epsilon) + decay_rate * master
    )
    master_new = master - step_rate * update
    return (master_new, first_new, second_new)


def on_device(
    key_grads,
    router_grads,
    gain_grads,
    key_master,
    key_first,
    key_second,
    router_master,
    router_first,
    router_second,
    gain_master,
    gain_first,
    gain_second,
):
    key_local = micro_total(key_grads)
    router_local = micro_total(router_grads)
    gain_local = micro_total(gain_grads)
    key_part, router_part, gain_part = (
        lax.psum_scatter(
            key_local.astype(jnp.bfloat16), "narrow", scatter_dimension=0, tiled=True
        ).astype(jnp.float32),
        lax.psum_scatter(
            router_local.astype(jnp.bfloat16), "narrow", scatter_dimension=1, tiled=True
        ).astype(jnp.float32),
        lax.psum_scatter(
            gain_local.astype(jnp.bfloat16), "narrow", scatter_dimension=0, tiled=True
        ).astype(jnp.float32),
    )
    key_sum, router_sum, gain_sum = lax.psum((key_part, router_part, gain_part), "wide")
    squares = (
        jnp.sum(key_sum * key_sum) + jnp.sum(router_sum * router_sum) + jnp.sum(gain_sum * gain_sum)
    )
    squares = lax.psum(squares, "narrow")
    clip_limit = 0.5 * math.sqrt(D * KEY_WIDTH + EXPERTS * D + D)
    factor = clip_limit / jnp.maximum(jnp.sqrt(squares), clip_limit)
    key_new, key_first_new, key_second_new = adamw(
        key_master, key_first, key_second, key_sum, factor, 0.1
    )
    router_new, router_first_new, router_second_new = adamw(
        router_master, router_first, router_second, router_sum, factor, 0.1
    )
    gain_new, gain_first_new, gain_second_new = adamw(
        gain_master, gain_first, gain_second, gain_sum, factor, 0.0
    )
    key_weight, router_weight, gain_weight = (
        lax.all_gather(key_new.astype(jnp.bfloat16), "narrow", axis=0, tiled=True),
        lax.all_gather(router_new.astype(jnp.bfloat16), "narrow", axis=1, tiled=True),
        lax.all_gather(gain_new.astype(jnp.bfloat16), "narrow", axis=0, tiled=True),
    )
    return (
        key_new,
        key_first_new,
        key_second_new,
        router_new,
        router_first_new,
        router_second_new,
        gain_new,
        gain_first_new,
        gain_second_new,
        key_weight,
        router_weight,
        gain_weight,
    )


def solution(mesh):
    in_specs = (
        P("wide", "narrow", None, None, None),
        P("wide", "narrow", None, None, None),
        P("wide", "narrow", None, None),
        P("narrow", None),
        P("narrow", None),
        P("narrow", None),
        P(None, "narrow"),
        P(None, "narrow"),
        P(None, "narrow"),
        P("narrow"),
        P("narrow"),
        P("narrow"),
    )
    out_specs = (
        P("narrow", None),
        P("narrow", None),
        P("narrow", None),
        P(None, "narrow"),
        P(None, "narrow"),
        P(None, "narrow"),
        P("narrow"),
        P("narrow"),
        P("narrow"),
        P(),
        P(),
        P(),
    )
    return jax.shard_map(
        on_device, mesh=mesh, in_specs=in_specs, out_specs=out_specs, check_vma=False
    )
```

profile of v0, /device:TPU:0, one launch (start us, length us, event | category | flops | bytes accessed | tf_op | source)
XLA Modules:
  0.0 194.4 jit_solution(306389804085520054)
XLA Ops:
  7.2 0.0 reduce-scatter.5.cloned.1.call-start
  7.2 1.9 reduce_sum.65
  9.1 0.0 reduce-scatter.5.cloned.1.call-update
  9.2 0.0 reduce-scatter.3.cloned.1.call-start
  9.2 4.9 %reduce_sum.63 = bf16[2048,512]{1,0:T(8,128)(2,1)} reduce(bf16[1,1,2,2048,512]{4,3,2,1,0:T(8,128)(2,1)} %param.12, bf16[]{:T(256)} %constant.13.clone.1), dimensions={0,1,2}, to_apply=%region_0.0 | reduce | flops 1048576 | bytes 6291458 | tf_op jit(solution)/shard_map/reduce_sum | solution.py:22
  14.1 0.0 copy-start.3
  14.1 0.0 copy-start.7
  14.1 0.0 reduce-scatter.3.cloned.1.call-update
  14.1 0.0 all-gather.2.cloned.1.call-start
  14.2 0.6 copy-done.3
  14.8 0.0 copy-done.7
  14.8 0.6 dynamic-slice
  16.1 5.9 %all-reduce = bf16[2048]{0:T(1024)(128)(2,1)S(1)} all-reduce(bf16[2048]{0:T(1024)(128)(2,1)S(1)} %reduce_sum.67), channel_id=4, replica_groups=mesh['wide'=16,'narrow'=2] {'narrow'}, use_global_device_ids=true, to_apply=%region_9.0.clone | all-reduce | flops 2048 | bytes 8192
  22.0 3.3 %reduce-scatter.5.cloned.1.call-done = bf16[64,1024]{1,0:T(8,128)(2,1)} async-done(((bf16[64,2048]{1,0:T(8,128)(2,1)}), bf16[64,1024]{1,0:T(8,128)(2,1)}) %reduce-scatter.5.cloned.1.call-update) | async-done | bytes 131088 | tf_op jit(solution)/shard_map/reduce_scatter | solution.py:59
  25.2 34.8 %reduce-scatter.3.cloned.1.call-done = bf16[1024,512]{1,0:T(8,128)(2,1)} async-done(((bf16[2048,512]{1,0:T(8,128)(2,1)}), bf16[1024,512]{1,0:T(8,128)(2,1)}) %reduce-scatter.3.cloned.1.call-update) | async-done | bytes 1048592 | tf_op jit(solution)/shard_map/reduce_scatter | solution.py:56
  60.1 76.1 %all-reduce.3 = (f32[1024,512]{1,0:T(8,128)S(1)}, f32[64,1024]{1,0:T(8,128)S(1)}, f32[1024]{0:T(1024)S(1)}) all-reduce(bf16[1024,512]{1,0:T(8,128)(2,1)} %reduce-scatter.3.cloned.1.call-done, bf16[64,1024]{1,0:T(8,128)(2,1)} %reduce-scatter.5.cloned.1.call-done, ...), channel_id=1, replica_groups=mesh['wide'=16,'narrow'=2] {'wide'}, use_global_device_ids=true, to_apply=%region_2.0 | all-reduce | flops 590848 | bytes 3547136 | tf_op jit(solution)/shard_map/psum | solution.py:66
  136.2 1.1 multiply_reduce_fusion
  137.3 0.7 multiply_reduce_fusion.1
  138.0 0.6 multiply_reduce_fusion.2
  140.6 5.4 %psum.31 = f32[]{:T(128)} all-reduce(f32[]{:T(128)S(6)} %add.66), channel_id=1, replica_groups=mesh['wide'=16,'narrow'=2] {'narrow'}, use_global_device_ids=true, to_apply=%region_12.0 | all-reduce | flops 1 | bytes 8 | tf_op jit(solution)/shard_map/psum | solution.py:70
  146.7 0.0 copy-start
  146.7 0.0 copy-start.1
  146.8 0.0 copy-start.2
  146.8 7.2 %fusion.7 = (bf16[1024,512]{1,0:T(8,128)(2,1)}, f32[1024,512]{1,0:T(8,128)}, f32[1024,512]{1,0:T(8,128)}, f32[1024,512]{1,0:T(8,128)}) fusion(f32[1024,512]{1,0:T(8,128)} %param.15, f32[1024,512]{1,0:T(8,128)S(1)} %get-tuple-element.12, f32[]{:T(128)S(6)} %div.48, f32[1024,512]{1,0:T(8,128)} %param.16, f32[1024,512]{1,0:T(8,128)} %param.17), kind=kLoop, calls=%fused_computation.18 | loop fusion | flops 8912896 | bytes 15728644 | tf_op jit(solution)/shard_map/convert_element_type | solution.py:83
  153.9 0.0 copy-start.4
  153.9 0.0 copy-start.5
  153.9 0.0 copy-start.6
  153.9 0.0 all-gather.2.cloned.1.call-update
  154.0 0.0 copy-done
  154.0 0.0 copy-done.1
  154.0 0.0 copy-done.2
  154.0 1.0 fusion.5
  155.0 5.6 %all_gather.10 = bf16[64,2048]{1,0:T(8,128)(2,1)S(1)} all-gather(bf16[64,1024]{1,0:T(8,128)(2,1)S(1)} %get-tuple-element.19), channel_id=1, replica_groups=mesh['wide'=16,'narrow'=2] {'narrow'}, dimensions={1}, use_global_device_ids=true | all-gather | bytes 393216 | tf_op jit(solution)/shard_map/all_gather | solution.py:84
  160.6 0.0 copy-done.4
  160.6 0.0 copy-done.5
  160.6 0.0 copy-done.6
  160.7 0.6 fusion.3
  161.3 4.3 %all_gather.11 = bf16[2048]{0:T(1024)(128)(2,1)S(1)} all-gather(bf16[1024]{0:T(1024)(128)(2,1)S(1)} %get-tuple-element.15), channel_id=1, replica_groups=mesh['wide'=16,'narrow'=2] {'narrow'}, dimensions={0}, use_global_device_ids=true | all-gather | bytes 6144 | tf_op jit(solution)/shard_map/all_gather | solution.py:85
  165.6 18.0 %all-gather.2.cloned.1.call-done = bf16[2048,512]{1,0:T(8,128)(2,1)} async-done(((bf16[1024,512]{1,0:T(8,128)(2,1)}), bf16[2048,512]{1,0:T(8,128)(2,1)}) %all-gather.2.cloned.1.call-update) | async-done | bytes 2097168 | tf_op jit(solution)/shard_map/all_gather | solution.py:83
  183.6 3.0 %copy.32 = bf16[2048,512]{1,0:T(8,128)(2,1)} copy(bf16[2048,512]{1,0:T(8,128)(2,1)} %all-gather.2.cloned.1.call-done) | data formatting | bytes 4194304
  186.6 0.7 copy.33
  187.3 0.6 copy.34
  (2 shorter events, 0.0 us)
Async XLA Ops:
  7.2 18.1 %reduce-scatter.5.cloned.1.call-start = ((), (), s32[]{:S(2)}) async-start(), calls=%async_computation.3 | async-start | bytes 393216 | tf_op jit(solution)/shard_map/reduce_scatter | solution.py:59
  9.2 50.9 %reduce-scatter.3.cloned.1.call-start = ((), (), s32[]{:S(2)}) async-start(), calls=%async_computation.2 | async-start | bytes 3145728 | tf_op jit(solution)/shard_map/reduce_scatter | solution.py:56
  14.1 0.7 copy-start.3
  14.1 0.7 copy-start.7
  14.1 169.4 %all-gather.2.cloned.1.call-start = ((), (), s32[]{:S(2)}) async-start(), calls=%async_computation.4 | async-start | bytes 3145728 | tf_op jit(solution)/shard_map/all_gather | solution.py:83
  146.7 7.2 %copy-start = (f32[64,1024]{1,0:T(8,128)S(1)}, f32[64,1024]{1,0:T(8,128)}, u32[]{:S(2)}) copy-start(f32[64,1024]{1,0:T(8,128)} %param.18) | copy-start | bytes 786436
  146.7 7.2 %copy-start.1 = (f32[64,1024]{1,0:T(8,128)S(1)}, f32[64,1024]{1,0:T(8,128)}, u32[]{:S(2)}) copy-start(f32[64,1024]{1,0:T(8,128)} %param.19) | copy-start | bytes 786436
  146.8 7.2 %copy-start.2 = (f32[64,1024]{1,0:T(8,128)S(1)}, f32[64,1024]{1,0:T(8,128)}, u32[]{:S(2)}) copy-start(f32[64,1024]{1,0:T(8,128)} %param.20) | copy-start | bytes 786436
  153.9 6.7 %copy-start.4 = (f32[1024]{0:T(1024)S(1)}, f32[1024]{0:T(1024)}, u32[]{:S(2)}) copy-start(f32[1024]{0:T(1024)} %param.21) | copy-start | bytes 12292
  153.9 6.7 %copy-start.5 = (f32[1024]{0:T(1024)S(1)}, f32[1024]{0:T(1024)}, u32[]{:S(2)}) copy-start(f32[1024]{0:T(1024)} %param.22) | copy-start | bytes 12292
  153.9 6.7 %copy-start.6 = (f32[1024]{0:T(1024)S(1)}, f32[1024]{0:T(1024)}, u32[]{:S(2)}) copy-start(f32[1024]{0:T(1024)} %param.23) | copy-start | bytes 12292
Sparse Core Ops, SparseCore 0:
  10.8 14.3 reduce-scatter.4
  28.1 31.8 reduce-scatter.2
  154.1 29.4 all-gather.1
where the time goes:
time: 195 us; the launch traced here: 194 us
  blocking collectives  97.4 us (50%)
  waiting for transfers between devices  56.1 us (29%)
  other arithmetic  18 us (9%)
  between operations  17.2 us (9%)
  local copies, waits for them, and re-layouts  5.57 us (3%)
    psum x1, blocking collectives, on_device(): lax.psum((key_part, router_part, gain_part), 'wide')  76.1 us
    reduce_scatter x1, waiting for transfers between devices, on_device(): lax.psum_scatter(key_local.astype(jnp.bfloat16), 'narrow', scatter_dimens...  34.8 us
    all_gather x1, waiting for transfers between devices, on_device(): lax.all_gather(key_new.astype(jnp.bfloat16), 'narrow', axis=0, tiled=True)  18 us
    convert_element_type x1, other arithmetic, on_device(): key_new.astype(jnp.bfloat16)  7.17 us
    reduce_sum x3, other arithmetic, micro_total(): summed = jnp.sum(grad_stack[0, 0].astype(jnp.float32), axis=0)  6.84 us
    unnamed x1, blocking collectives  5.89 us
    all_gather x1, blocking collectives, on_device(): lax.all_gather(router_new.astype(jnp.bfloat16), 'narrow', axis=1, tiled=T...  5.63 us
    unnamed x20, local copies, waits for them, and re-layouts  5.57 us
  transfers between devices with their start and end apart: 3, of which 3 were waited for; matrix products, arithmetic and copies ran while one was open for 4% of the time, Pallas kernels for 0%

commit v1 on v0

v1 whole, which is shorter than its diff:
```python
import functools
import math

import jax
import jax.numpy as jnp
from jax import lax
from jax.experimental import pallas as pl
from jax.experimental.pallas import tpu as pltpu
from jax.sharding import PartitionSpec as P

beta_one = 0.9
beta_two = 0.95
step_rate = 0.01
epsilon = 1e-08
bias_one = 1.0 - 0.9**10
bias_two = 1.0 - 0.95**10

LANES = 256
PARTS = 3
HALVED_BITS = 4
F32, BF16 = jnp.float32, jnp.bfloat16


def adamw(master, first_moment, second, gradient, factor, decay_rate):
    scaled = factor * gradient
    first_new = beta_one * first_moment + (1.0 - beta_one) * scaled
    second_new = beta_two * second + (1.0 - beta_two) * scaled * scaled
    update = (
        first_new / bias_one / (jnp.sqrt(second_new / bias_two) + epsilon) + decay_rate * master
    )
    master_new = master - step_rate * update
    return (master_new, first_new, second_new)


def rows_loop(count, step, body):
    def one(i, carry):
        body(pl.multiple_of(i * step, 16))
        return carry

    lax.fori_loop(0, count // step, one, 0)


def layout(key_shape, router_shape):
    half_rows, half_cols = key_shape[0] // 2, router_shape[1] // 2
    blocks, at = [], 0
    for col in range(0, key_shape[1], LANES):
        blocks.append((at, half_rows, "key", col))
        at += half_rows
    for col in range(0, half_cols, LANES):
        blocks.append((at, router_shape[0], "router", col))
        at += router_shape[0]
    return blocks, at


def part_orders():
    return (("x", 1, 2), (1, 2, "x"), (2, "x", 1))


def stage_shapes(part_rows, wide_bits):
    plans = []
    for order in part_orders():
        halves, count, plan = 2, part_rows, []
        for axis in (0,) + order + (3,):
            if axis == "x":
                halves = 1
            else:
                count //= 2
            plan.append((axis, (halves, count, LANES)))
        for axis in range(HALVED_BITS, wide_bits):
            plan.append((axis, (halves, count, LANES)))
        plans.append(plan)
    return plans


def reduce_kernel(
    plans,
    blocks,
    total_rows,
    clip_limit,
    key_ref,
    router_ref,
    gain_ref,
    key_out,
    router_out,
    gain_out,
    factor_out,
    local,
    acc,
    full,
    gain_val,
    gain_in,
    square_val,
    square_in,
    send_bufs,
    recv_bufs,
    send_sem,
    recv_sem,
    gather_send,
    gather_recv,
    gain_send,
    gain_recv,
    square_send,
    square_recv,
):
    wide, narrow = lax.axis_index("wide"), lax.axis_index("narrow")
    stages = len(plans[0])
    part_rows = total_rows // PARTS
    wide_bits = stages - 1
    bit = [(wide // 2**k) % 2 for k in range(wide_bits)]

    def partner(axis):
        if axis == "x":
            return (wide, 1 - narrow)
        return (wide + (1 - 2 * bit[axis]) * 2**axis, narrow)

    diagonal = (partner(3)[0], 1 - narrow)
    friends = [partner(a) for a in ["x"] + list(range(wide_bits))] + [diagonal]
    barrier = pltpu.get_barrier_semaphore()
    for friend in friends:
        pl.semaphore_signal(barrier, inc=1, device_id=friend, device_id_type=pl.DeviceIdType.MESH)
    pl.semaphore_wait(barrier, len(friends))

    def remote(src, dst, send, recv, to):
        return pltpu.make_async_remote_copy(
            src_ref=src,
            dst_ref=dst,
            send_sem=send,
            recv_sem=recv,
            device_id=to,
            device_id_type=pl.DeviceIdType.MESH,
        )

    started = []
    gain_copies = []

    def send_gain(stage):
        copy = remote(
            gain_val.at[stage],
            gain_in.at[stage],
            gain_send.at[stage],
            gain_recv.at[stage],
            partner(plans[0][stage][0]),
        )
        copy.start()
        gain_copies.append(copy)

    gain_local = jnp.sum(gain_ref[0, 0].astype(F32), axis=0, keepdims=True)
    gain_val[0] = gain_local.astype(BF16).astype(F32)
    send_gain(0)
    copies = []
    for p in range(PARTS):
        low, high = p * part_rows, (p + 1) * part_rows
        for half in range(2):
            for at, count, kind, col in blocks:
                start, stop = max(at, low), min(at + count, high)
                if start >= stop:
                    continue

                def fill(r, half=half, at=at, start=start, kind=kind, col=col):
                    if kind == "key":
                        first = pl.multiple_of(half * count_key + start - at + r, 16)
                        rows, cols = pl.ds(first, 64), slice(col, col + LANES)
                        source = key_ref
                    else:
                        first = pl.multiple_of(start - at + r, 16)
                        left = half * count_router + col
                        rows, cols = pl.ds(first, 64), slice(left, left + LANES)
                        source = router_ref
                    one = source[0, 0, 0, rows, cols].astype(F32)
                    two = source[0, 0, 1, rows, cols].astype(F32)
                    into = pl.ds(pl.multiple_of(start + r, 16), 64)
                    local[half, into, :] = (one + two).astype(BF16)

                count_key = key_ref.shape[3] // 2
                count_router = router_ref.shape[4] // 2
                rows_loop(stop - start, 64, fill)
        count = part_rows // 2
        sent = pl.multiple_of(low + (1 - bit[0]) * count, 16)
        copy = remote(
            local.at[:, pl.ds(sent, count), :],
            recv_bufs[p][0],
            send_sem.at[p, 0],
            recv_sem.at[p, 0],
            partner(0),
        )
        copy.start()
        copies.append(copy)
        started.append(copy)

    base = [pl.multiple_of(p * part_rows + bit[0] * (part_rows // 2), 16) for p in range(PARTS)]
    rows_now = [part_rows // 2] * PARTS
    split = [False] * PARTS

    def add(p, stage, half, h, offset, r, step):
        previous = local if stage == 0 else acc
        mine = previous[half, pl.ds(pl.multiple_of(base[p] + offset + r, 16), step), :]
        theirs = recv_bufs[p][stage][h, pl.ds(pl.multiple_of(offset + r, 16), step), :]
        return mine.astype(F32) + theirs.astype(F32)

    for stage in range(1, stages):
        gain_copies[stage - 1].wait_recv()
        gain_val[stage] = gain_val[stage - 1] + gain_in[stage - 1]
        send_gain(stage)
        fresh = []
        for p in range(PARTS):
            axis, shape = plans[p][stage]
            copies[p].wait_recv()
            halves = [(narrow, 0)] if split[p] else [(0, 0), (1, 1)]
            send_buf = send_bufs[p][stage - 1]
            step = 48
            if axis == "x":
                send_sets, keep_sets = [(1 - narrow, 1 - narrow, 0)], [(narrow, narrow)]
                send_offset = keep_offset = 0
            elif axis < HALVED_BITS:
                send_sets = [(half, h, h) for half, h in halves]
                keep_sets = halves
                send_offset = (1 - bit[axis]) * shape[1]
                keep_offset = bit[axis] * shape[1]
            else:
                send_sets, keep_sets = [(narrow, 0, 0)], []
                send_offset = keep_offset = 0

            def out(r, p=p):
                for half, h, slot in send_sets:
                    value = add(p, stage - 1, half, h, send_offset, r, step)
                    send_buf[slot, pl.ds(r, step), :] = value.astype(BF16)
                    if not keep_sets:
                        rows = pl.ds(pl.multiple_of(base[p] + r, 16), step)
                        acc[half, rows, :] = value.astype(BF16).astype(F32)

            rows_loop(shape[1], step, out)
            copy = remote(
                send_buf,
                recv_bufs[p][stage],
                send_sem.at[p, stage],
                recv_sem.at[p, stage],
                partner(axis),
            )
            copy.start()
            fresh.append(copy)
            started.append(copy)

            def keep(r, p=p):
                for half, h in keep_sets:
                    value = add(p, stage - 1, half, h, keep_offset, r, step)
                    rows = pl.ds(pl.multiple_of(base[p] + keep_offset + r, 16), step)
                    acc[half, rows, :] = value

            if keep_sets:
                rows_loop(shape[1], step, keep)
            if axis == "x":
                split[p] = True
            base[p] = pl.multiple_of(base[p] + keep_offset, 16)
            rows_now[p] = shape[1]
        copies = fresh

    gather_axes = [
        [3] + [a for a in reversed(part_orders()[p]) if a != "x"] + [0] for p in range(PARTS)
    ]
    gathers = []

    def gather(p, stage):
        rows = pl.ds(base[p], rows_now[p])
        axis = gather_axes[p][stage]
        copy = remote(
            full.at[rows, :],
            full.at[rows, :],
            gather_send.at[p, stage],
            gather_recv.at[p, stage],
            partner(axis),
        )
        copy.start()
        started.append(copy)
        base[p] = pl.multiple_of(base[p] - bit[axis] * rows_now[p], 16)
        rows_now[p] = 2 * rows_now[p]
        return copy

    squares = jnp.zeros((8, LANES), F32)
    for p in range(PARTS):
        copies[p].wait_recv()
        count = rows_now[p]
        value = add(p, stages - 1, narrow, 0, 0, 0, count)
        full[pl.ds(base[p], count), :] = value.astype(BF16)
        gathers.append(gather(p, 0))
        squares = squares + jnp.sum((value * value).reshape(count // 8, 8, LANES), axis=0)

    def send_square(source, slot, to):
        copy = remote(
            square_val.at[source],
            square_in.at[slot],
            square_send.at[slot],
            square_recv.at[slot],
            to,
        )
        copy.start()
        started.append(copy)
        return copy

    square_val[0] = squares
    square_copies = [
        send_square(0, 0, partner("x")),
        send_square(0, 1, partner(3)),
        send_square(0, 2, diagonal),
    ]
    gain_copies[stages - 1].wait_recv()
    gain_sum = gain_val[stages - 1] + gain_in[stages - 1]
    gain_val[stages] = gain_sum
    left = pl.multiple_of(narrow * gain_out.shape[1], 128)
    gain_out[...] = gain_val[stages, :, pl.ds(left, gain_out.shape[1])]
    for copy in square_copies:
        copy.wait_recv()
    square_val[1] = (square_val[0] + square_in[0]) + (square_in[1] + square_in[2])
    for stage in range(1, 4):
        square_copy = send_square(stage, stage + 2, partner((2, 1, 0)[stage - 1]))
        for p in range(PARTS):
            gathers[p].wait_recv()
            gathers[p] = gather(p, stage)
        square_copy.wait_recv()
        square_val[stage + 1] = square_val[stage] + square_in[stage + 2]
    total = jnp.sum(square_val[4]) + jnp.sum(gain_sum * gain_sum)
    total = jnp.full(factor_out.shape, total, F32)
    factor_out[...] = clip_limit / jnp.maximum(jnp.sqrt(total), clip_limit)
    for copy in gathers:
        copy.wait_recv()
    for at, count, kind, col in blocks:
        target = key_out if kind == "key" else router_out

        def place(r, at=at, col=col, target=target):
            rows = pl.ds(pl.multiple_of(at + r, 16), 64)
            target[pl.ds(r, 64), col : col + LANES] = full[rows, :]

        rows_loop(count, 64, place)
    for copy in started + gain_copies:
        copy.wait_send()


def reduce_grads(wide_size, key_grads, router_grads, gain_grads):
    key_shape, router_shape = key_grads.shape[3:], router_grads.shape[3:]
    gain_size = gain_grads.shape[3]
    blocks, total_rows = layout(key_shape, router_shape)
    wide_bits = wide_size.bit_length() - 1
    plans = stage_shapes(total_rows // PARTS, wide_bits)
    stages = len(plans[0])
    count = math.prod(key_shape) + math.prod(router_shape) + gain_size
    vmem = pl.BlockSpec(memory_space=pltpu.VMEM)
    return pl.pallas_call(
        functools.partial(
            reduce_kernel, plans, blocks, total_rows, 0.5 * math.sqrt(count)
        ),
        out_shape=(
            jax.ShapeDtypeStruct((key_shape[0] // 2, key_shape[1]), BF16),
            jax.ShapeDtypeStruct((router_shape[0], router_shape[1] // 2), BF16),
            jax.ShapeDtypeStruct((1, gain_size // 2), F32),
            jax.ShapeDtypeStruct((1, 128), F32),
        ),
        in_specs=[vmem] * 3,
        out_specs=(vmem,) * 4,
        scratch_shapes=[
            pltpu.VMEM((2, total_rows, LANES), BF16),
            pltpu.VMEM((2, total_rows, LANES), F32),
            pltpu.VMEM((total_rows, LANES), BF16),
            pltpu.VMEM((stages + 1, 1, gain_size), F32),
            pltpu.VMEM((stages, 1, gain_size), F32),
            pltpu.VMEM((5, 8, LANES), F32),
            pltpu.VMEM((6, 8, LANES), F32),
            [[pltpu.VMEM(shape, BF16) for _, shape in plan[1:]] for plan in plans],
            [[pltpu.VMEM(shape, BF16) for _, shape in plan] for plan in plans],
            pltpu.SemaphoreType.DMA((PARTS, stages)),
            pltpu.SemaphoreType.DMA((PARTS, stages)),
            pltpu.SemaphoreType.DMA((PARTS, 4)),
            pltpu.SemaphoreType.DMA((PARTS, 4)),
            pltpu.SemaphoreType.DMA((stages,)),
            pltpu.SemaphoreType.DMA((stages,)),
            pltpu.SemaphoreType.DMA((6,)),
            pltpu.SemaphoreType.DMA((6,)),
        ],
        compiler_params=pltpu.CompilerParams(
            collective_id=0, has_side_effects=True, vmem_limit_bytes=40 * 2**20
        ),
    )(key_grads, router_grads, gain_grads)


def on_device(
    wide_size,
    key_grads,
    router_grads,
    gain_grads,
    key_master,
    key_first,
    key_second,
    router_master,
    router_first,
    router_second,
    gain_master,
    gain_first,
    gain_second,
):
    key_sum, router_sum, gain_sum, factor = reduce_grads(
        wide_size, key_grads, router_grads, gain_grads
    )
    key_sum, router_sum = key_sum.astype(F32), router_sum.astype(F32)
    gain_sum, factor = gain_sum[0], factor[0, 0]
    key_new, key_first_new, key_second_new = adamw(
        key_master, key_first, key_second, key_sum, factor, 0.1
    )
    router_new, router_first_new, router_second_new = adamw(
        router_master, router_first, router_second, router_sum, factor, 0.1
    )
    gain_new, gain_first_new, gain_second_new = adamw(
        gain_master, gain_first, gain_second, gain_sum, factor, 0.0
    )
    key_weight, router_weight, gain_weight = (
        lax.all_gather(key_new.astype(BF16), "narrow", axis=0, tiled=True),
        lax.all_gather(router_new.astype(BF16), "narrow", axis=1, tiled=True),
        lax.all_gather(gain_new.astype(BF16), "narrow", axis=0, tiled=True),
    )
    return (
        key_new,
        key_first_new,
        key_second_new,
        router_new,
        router_first_new,
        router_second_new,
        gain_new,
        gain_first_new,
        gain_second_new,
        key_weight,
        router_weight,
        gain_weight,
    )


def solution(mesh):
    state = (P("narrow", None),) * 3 + (P(None, "narrow"),) * 3 + (P("narrow"),) * 3
    grads = (
        P("wide", "narrow", None, None, None),
        P("wide", "narrow", None, None, None),
        P("wide", "narrow", None, None),
    )
    return jax.shard_map(
        functools.partial(on_device, mesh.shape["wide"]),
        mesh=mesh,
        in_specs=grads + state,
        out_specs=state + (P(), P(), P()),
        check_vma=False,
    )
```

time: 195 us -> 101 us (0.52)
  blocking collectives: 97.4 us -> 11.1 us
  Pallas kernels: 0 us -> 40.9 us
  waiting for transfers between devices: 56.1 us -> 18.6 us
  other arithmetic: 18 us -> 7.66 us
  between operations: 17.2 us -> 14.2 us
  local copies, waits for them, and re-layouts: 5.57 us -> 8.29 us
    psum x2 -> x0, blocking collectives: 81.6 us -> none  [the longest x1 76.1 us: on_device(): lax.psum((key_part, router_part, gain_part), 'wide')]
    pallas_call x0 -> x1, Pallas kernels: none -> 40.9 us  [reduce_grads(): pl.pallas_call(functools.partial(reduce_kernel, plans, blocks, total_rows...]
    reduce_scatter x2 -> x0, waiting for transfers between devices: 38.1 us -> none  [the longest x1 34.8 us: on_device(): lax.psum_scatter(key_local.astype(jnp.bfloat16), 'narrow', scatter_dimens...]
    reduce_sum x6 -> x0, other arithmetic: 9.24 us -> none  [the longest x3 6.84 us: micro_total(): summed = jnp.sum(grad_stack[0, 0].astype(jnp.float32), axis=0)]
    unnamed x1 -> x0, blocking collectives: 5.89 us -> none
    unnamed x20 -> x25, local copies, waits for them, and re-layouts: 5.57 us -> 8.29 us
    convert_element_type x4 -> x3, other arithmetic: 8.8 us -> 7.62 us  [the longest x1 5.95 us: on_device(): key_new.astype(BF16)]
  transfers between devices with their start and end apart: 3 -> 1, of which waited for: 3 -> 1; matrix products, arithmetic and copies ran while one was open for 4% -> 2% of each run, Pallas kernels for 0% -> 0%
where the time goes in v1:
time: 101 us
  Pallas kernels  40.9 us (40%)
  waiting for transfers between devices  18.6 us (18%)
  between operations  14.2 us (14%)
  blocking collectives  11.1 us (11%)
  local copies, waits for them, and re-layouts  8.29 us (8%)
  other arithmetic  7.66 us (8%)
    pallas_call x1, Pallas kernels, reduce_grads(): pl.pallas_call(functools.partial(reduce_kernel, plans, blocks, total_rows...  40.9 us
    all_gather x1, waiting for transfers between devices, on_device(): lax.all_gather(key_new.astype(BF16), 'narrow', axis=0, tiled=True)  18.5 us
    unnamed x25, local copies, waits for them, and re-layouts  8.29 us
    all_gather x1, blocking collectives, on_device(): lax.all_gather(router_new.astype(BF16), 'narrow', axis=1, tiled=True)  6.71 us
    convert_element_type x1, other arithmetic, on_device(): key_new.astype(BF16)  5.95 us
    all_gather x1, blocking collectives, on_device(): lax.all_gather(gain_new.astype(BF16), 'narrow', axis=0, tiled=True)  4.34 us
  transfers between devices with their start and end apart: 1, of which 1 were waited for; matrix products, arithmetic and copies ran while one was open for 2% of the time, Pallas kernels for 0%

profile of v1, /device:TPU:0, one launch (start us, length us, event | category | flops | bytes accessed | tf_op | source)
XLA Modules:
  0.0 100.7 jit_solution(10627690315094327874)
XLA Ops:
  7.2 0.0 all-gather.2.cloned.1.call-start
  7.2 0.0 copy-start
  7.2 2.2 %copy-done = bf16[1,1,2,2048,512]{4,3,2,1,0:T(8,128)(2,1)S(1)} copy-done((bf16[1,1,2,2048,512]{4,3,2,1,0:T(8,128)(2,1)S(1)}, bf16[1,1,2,2048,512]{4,3,2,1,0:T(8,128)(2,1)}, u32[]{:S(2)}) %copy-start) | copy-done | bytes 4194328
  9.4 0.0 copy-start.1
  9.4 1.0 %copy-done.1 = bf16[1,1,2,64,2048]{4,3,2,1,0:T(8,128)(2,1)S(1)} copy-done((bf16[1,1,2,64,2048]{4,3,2,1,0:T(8,128)(2,1)S(1)}, bf16[1,1,2,64,2048]{4,3,2,1,0:T(8,128)(2,1)}, u32[]{:S(2)}) %copy-start.1) | copy-done | bytes 524312
  10.5 0.0 copy-start.2
  10.5 0.7 copy-done.2
  11.2 0.0 copy-start.3
  11.2 0.0 copy-start.4
  11.2 40.9 %shard_map.211 = (bf16[1024,512]{1,0:T(8,128)(2,1)S(1)}, bf16[64,1024]{1,0:T(8,128)(2,1)S(1)}, f32[1,1024]{1,0:T(1,128)S(1)}, f32[1,128]{1,0:T(1,128)S(1)}) custom-call(bf16[1,1,2,2048,512]{4,3,2,1,0:T(8,128)(2,1)S(1)} %copy-done, bf16[1,1,2,64,2048]{4,3,2,1,0:T(8,128)(2,1)S(1)} %copy-done.1, bf16[1,1,2,2048]{3,2,1,0:T(2,128)(2,1)S(1)} %copy-done.2), custom_call_target="tpu_custom_call" | custom-call | tf_op jit(solution)/shard_map/pallas_call | solution.py:346
  52.1 0.0 copy-done.3
  52.1 0.0 copy-done.4
  52.1 0.0 copy-start.5
  52.1 0.0 copy-start.6
  52.1 0.0 copy-start.7
  52.2 5.9 %fusion.7 = (bf16[1024,512]{1,0:T(8,128)(2,1)}, f32[1024,512]{1,0:T(8,128)}, f32[1024,512]{1,0:T(8,128)}, f32[1024,512]{1,0:T(8,128)}) fusion(f32[1024,512]{1,0:T(8,128)S(1)} %copy-done.3, bf16[1024,512]{1,0:T(8,128)(2,1)S(1)} %get-tuple-element.17, f32[]{:T(128)S(1)} %bitcast.3, f32[1024,512]{1,0:T(8,128)S(1)} %copy-done.4, f32[1024,512]{1,0:T(8,128)} %param.17), kind=kLoop, calls=%fused_computation.17 | loop fusion | flops 9437184 | bytes 14680068 | tf_op jit(solution)/shard_map/convert_element_type | solution.py:413
  58.1 0.0 copy-start.8
  58.1 0.0 copy-start.9
  58.1 0.0 copy-start.10
  58.1 0.0 all-gather.2.cloned.1.call-update
  58.1 0.0 copy-done.5
  58.1 0.0 copy-done.6
  58.2 0.0 copy-done.7
  58.2 1.1 %fusion.5 = (bf16[64,1024]{1,0:T(8,128)(2,1)S(1)}, f32[64,1024]{1,0:T(8,128)}, f32[64,1024]{1,0:T(8,128)}, f32[64,1024]{1,0:T(8,128)}) fusion(f32[64,1024]{1,0:T(8,128)S(1)} %copy-done.5, bf16[64,1024]{1,0:T(8,128)(2,1)S(1)} %get-tuple-element.18, f32[]{:T(128)S(1)} %bitcast.4, f32[64,1024]{1,0:T(8,128)S(1)} %copy-done.6, f32[64,1024]{1,0:T(8,128)S(1)} %copy-done.7), kind=kLoop, calls=%fused_computation.16 | loop fusion | flops 1179648 | bytes 1835012 | tf_op jit(solution)/shard_map/convert_element_type | solution.py:414
  59.2 6.7 %all_gather.10 = bf16[64,2048]{1,0:T(8,128)(2,1)S(1)} all-gather(bf16[64,1024]{1,0:T(8,128)(2,1)S(1)} %get-tuple-element.24), channel_id=1, replica_groups=mesh['wide'=16,'narrow'=2] {'narrow'}, dimensions={1}, use_global_device_ids=true | all-gather | bytes 393216 | tf_op jit(solution)/shard_map/all_gather | solution.py:414
  66.0 0.0 copy-done.8
  66.0 0.0 copy-done.9
  66.0 0.0 copy-done.10
  66.0 0.6 fusion.3
  66.6 4.3 %all_gather.11 = bf16[2048]{0:T(1024)(128)(2,1)S(1)} all-gather(bf16[1024]{0:T(1024)(128)(2,1)S(1)} %get-tuple-element.20), channel_id=1, replica_groups=mesh['wide'=16,'narrow'=2] {'narrow'}, dimensions={0}, use_global_device_ids=true | all-gather | bytes 6144 | tf_op jit(solution)/shard_map/all_gather | solution.py:415
  71.0 18.5 %all-gather.2.cloned.1.call-done = bf16[2048,512]{1,0:T(8,128)(2,1)} async-done(((bf16[1024,512]{1,0:T(8,128)(2,1)}), bf16[2048,512]{1,0:T(8,128)(2,1)}) %all-gather.2.cloned.1.call-update) | async-done | bytes 2097168 | tf_op jit(solution)/shard_map/all_gather | solution.py:413
  89.5 3.0 %copy.27 = bf16[2048,512]{1,0:T(8,128)(2,1)} copy(bf16[2048,512]{1,0:T(8,128)(2,1)} %all-gather.2.cloned.1.call-done) | data formatting | bytes 4194304
  92.5 0.7 copy.28
  93.2 0.6 copy.29
  (1 shorter events, 0.0 us)
Async XLA Ops:
  7.2 82.3 %all-gather.2.cloned.1.call-start = ((), (), s32[]{:S(2)}) async-start(), calls=%async_computation | async-start | bytes 3145728 | tf_op jit(solution)/shard_map/all_gather | solution.py:413
  7.2 2.2 %copy-start = (bf16[1,1,2,2048,512]{4,3,2,1,0:T(8,128)(2,1)S(1)}, bf16[1,1,2,2048,512]{4,3,2,1,0:T(8,128)(2,1)}, u32[]{:S(2)}) copy-start(bf16[1,1,2,2048,512]{4,3,2,1,0:T(8,128)(2,1)} %key_ref.1) | copy-start | bytes 12582916
  9.4 1.0 %copy-start.1 = (bf16[1,1,2,64,2048]{4,3,2,1,0:T(8,128)(2,1)S(1)}, bf16[1,1,2,64,2048]{4,3,2,1,0:T(8,128)(2,1)}, u32[]{:S(2)}) copy-start(bf16[1,1,2,64,2048]{4,3,2,1,0:T(8,128)(2,1)} %router_ref.1) | copy-start | bytes 1572868
  10.5 0.7 copy-start.2
  11.2 40.9 %copy-start.3 = (f32[1024,512]{1,0:T(8,128)S(1)}, f32[1024,512]{1,0:T(8,128)}, u32[]{:S(2)}) copy-start(f32[1024,512]{1,0:T(8,128)} %param.15) | copy-start | bytes 6291460
  11.2 41.0 %copy-start.4 = (f32[1024,512]{1,0:T(8,128)S(1)}, f32[1024,512]{1,0:T(8,128)}, u32[]{:S(2)}) copy-start(f32[1024,512]{1,0:T(8,128)} %param.16) | copy-start | bytes 6291460
  52.1 6.0 %copy-start.5 = (f32[64,1024]{1,0:T(8,128)S(1)}, f32[64,1024]{1,0:T(8,128)}, u32[]{:S(2)}) copy-start(f32[64,1024]{1,0:T(8,128)} %param.18) | copy-start | bytes 786436
  52.1 6.0 %copy-start.6 = (f32[64,1024]{1,0:T(8,128)S(1)}, f32[64,1024]{1,0:T(8,128)}, u32[]{:S(2)}) copy-start(f32[64,1024]{1,0:T(8,128)} %param.19) | copy-start | bytes 786436
  52.1 6.0 %copy-start.7 = (f32[64,1024]{1,0:T(8,128)S(1)}, f32[64,1024]{1,0:T(8,128)}, u32[]{:S(2)}) copy-start(f32[64,1024]{1,0:T(8,128)} %param.20) | copy-start | bytes 786436
  58.1 7.9 %copy-start.8 = (f32[1024]{0:T(1024)S(1)}, f32[1024]{0:T(1024)}, u32[]{:S(2)}) copy-start(f32[1024]{0:T(1024)} %param.21) | copy-start | bytes 12292
  58.1 7.9 %copy-start.9 = (f32[1024]{0:T(1024)S(1)}, f32[1024]{0:T(1024)}, u32[]{:S(2)}) copy-start(f32[1024]{0:T(1024)} %param.22) | copy-start | bytes 12292
  58.1 7.9 %copy-start.10 = (f32[1024]{0:T(1024)S(1)}, f32[1024]{0:T(1024)}, u32[]{:S(2)}) copy-start(f32[1024]{0:T(1024)} %param.23) | copy-start | bytes 12292
Sparse Core Ops, SparseCore 0:
  58.3 31.2 all-gather.1

commit v2 on v1

--- a/solution.py
+++ b/solution.py
@@ -18,6 +18,7 @@
 LANES = 256
 PARTS = 3
 HALVED_BITS = 4
+KEY_PIECE = 64
 F32, BF16 = jnp.float32, jnp.bfloat16
 
 
@@ -25,11 +26,11 @@
     scaled = factor * gradient
     first_new = beta_one * first_moment + (1.0 - beta_one) * scaled
     second_new = beta_two * second + (1.0 - beta_two) * scaled * scaled
-    update = (
-        first_new / bias_one / (jnp.sqrt(second_new / bias_two) + epsilon) + decay_rate * master
-    )
-    master_new = master - step_rate * update
-    return (master_new, first_new, second_new)
+    root = jnp.sqrt(second_new * (1.0 / bias_two)) + epsilon
+    update = first_new * (1.0 / bias_one) / root
+    if decay_rate:
+        update = update + decay_rate * master
+    return (master - step_rate * update, first_new, second_new)
 
 
 def rows_loop(count, step, body):
@@ -80,10 +81,18 @@
     key_ref,
     router_ref,
     gain_ref,
+    key_state,
+    router_state,
+    gain_state,
     key_out,
     router_out,
     gain_out,
     factor_out,
+    key_other,
+    router_other,
+    gain_other,
+    grads,
+    gain_grads,
     local,
     acc,
     full,
@@ -101,6 +110,21 @@
     gain_recv,
     square_send,
     square_recv,
+    key_mine,
+    router_mine,
+    gain_mine,
+    key_weight,
+    router_weight,
+    key_far,
+    router_far,
+    gain_new,
+    gain_far,
+    load_sem,
+    mine_sem,
+    weight_send,
+    weight_recv,
+    gain_far_sem,
+    out_sem,
 ):
     wide, narrow = lax.axis_index("wide"), lax.axis_index("narrow")
     stages = len(plans[0])
@@ -112,6 +136,42 @@
         if axis == "x":
             return (wide, 1 - narrow)
         return (wide + (1 - 2 * bit[axis]) * 2**axis, narrow)
+
+    half_rows, half_cols = key_ref.shape[3] // 2, router_ref.shape[4] // 2
+    gain_load = pltpu.make_async_copy(gain_ref.at[0, 0], gain_grads, load_sem.at[0])
+    gain_load.start()
+    loads = []
+    for p in range(PARTS):
+        part_loads = []
+        for half in range(2):
+            for at, count, kind, col in blocks:
+                start, stop = max(at, p * part_rows), min(at + count, (p + 1) * part_rows)
+                if start >= stop:
+                    continue
+                first = start - at + (half * half_rows if kind == "key" else 0)
+                left = col + (half * half_cols if kind == "router" else 0)
+                source = key_ref if kind == "key" else router_ref
+                copy = pltpu.make_async_copy(
+                    source.at[0, 0, :, pl.ds(first, stop - start), pl.ds(left, LANES)],
+                    grads.at[:, half, pl.ds(start, stop - start), :],
+                    load_sem.at[1 + len(part_loads) + sum(map(len, loads))],
+                )
+                copy.start()
+                part_loads.append(copy)
+        loads.append(part_loads)
+
+    quarter = 2 * bit[0] + bit[1]
+    key_rows, router_rows = half_rows // 4, router_ref.shape[3] // 4
+    mine_loads = []
+    for i, (state, mine, count) in enumerate(
+        [(r, key_mine, key_rows) for r in key_state]
+        + [(r, router_mine, router_rows) for r in router_state]
+        + [(r, gain_mine, 1) for r in gain_state]
+    ):
+        rows = pl.ds(pl.multiple_of(quarter * count, 16), count) if count > 1 else pl.ds(0, 1)
+        copy = pltpu.make_async_copy(state.at[rows, :], mine.at[i % 3], mine_sem.at[i])
+        copy.start()
+        mine_loads.append(copy)
 
     diagonal = (partner(3)[0], 1 - narrow)
     friends = [partner(a) for a in ["x"] + list(range(wide_bits))] + [diagonal]
@@ -144,38 +204,25 @@
         copy.start()
         gain_copies.append(copy)
 
-    gain_local = jnp.sum(gain_ref[0, 0].astype(F32), axis=0, keepdims=True)
+    gain_load.wait()
+    gain_local = jnp.sum(gain_grads[...].astype(F32), axis=0, keepdims=True)
     gain_val[0] = gain_local.astype(BF16).astype(F32)
     send_gain(0)
     copies = []
     for p in range(PARTS):
-        low, high = p * part_rows, (p + 1) * part_rows
-        for half in range(2):
-            for at, count, kind, col in blocks:
-                start, stop = max(at, low), min(at + count, high)
-                if start >= stop:
-                    continue
-
-                def fill(r, half=half, at=at, start=start, kind=kind, col=col):
-                    if kind == "key":
-                        first = pl.multiple_of(half * count_key + start - at + r, 16)
-                        rows, cols = pl.ds(first, 64), slice(col, col + LANES)
-                        source = key_ref
-                    else:
-                        first = pl.multiple_of(start - at + r, 16)
-                        left = half * count_router + col
-                        rows, cols = pl.ds(first, 64), slice(left, left + LANES)
-                        source = router_ref
-                    one = source[0, 0, 0, rows, cols].astype(F32)
-                    two = source[0, 0, 1, rows, cols].astype(F32)
-                    into = pl.ds(pl.multiple_of(start + r, 16), 64)
-                    local[half, into, :] = (one + two).astype(BF16)
-
-                count_key = key_ref.shape[3] // 2
-                count_router = router_ref.shape[4] // 2
-                rows_loop(stop - start, 64, fill)
+        for load in loads[p]:
+            load.wait()
         count = part_rows // 2
-        sent = pl.multiple_of(low + (1 - bit[0]) * count, 16)
+        sent = pl.multiple_of(p * part_rows + (1 - bit[0]) * count, 16)
+        kept = pl.multiple_of(p * part_rows + bit[0] * count, 16)
+
+        def fill(r, first):
+            rows = pl.ds(pl.multiple_of(first + r, 16), 48)
+            for half in range(2):
+                one, two = grads[0, half, rows, :], grads[1, half, rows, :]
+                local[half, rows, :] = (one.astype(F32) + two.astype(F32)).astype(BF16)
+
+        rows_loop(count, 48, functools.partial(fill, first=sent))
         copy = remote(
             local.at[:, pl.ds(sent, count), :],
             recv_bufs[p][0],
@@ -186,6 +233,7 @@
         copy.start()
         copies.append(copy)
         started.append(copy)
+        rows_loop(count, 48, functools.partial(fill, first=kept))
 
     base = [pl.multiple_of(p * part_rows + bit[0] * (part_rows // 2), 16) for p in range(PARTS)]
     rows_now = [part_rows // 2] * PARTS
@@ -322,19 +370,197 @@
     factor_out[...] = clip_limit / jnp.maximum(jnp.sqrt(total), clip_limit)
     for copy in gathers:
         copy.wait_recv()
+    for copy in mine_loads:
+        copy.wait()
+
+    factor = factor_out[0:1, 0:1]
+    gain_new[...] = adamw(
+        gain_mine[0], gain_mine[1], gain_mine[2], gain_out[...], factor, 0.0
+    )[0]
+    gain_copy = remote(gain_new, gain_far, gain_far_sem.at[0], gain_far_sem.at[1], partner("x"))
+    gain_copy.start()
+    pieces = [("key", i * KEY_PIECE, KEY_PIECE) for i in range(key_rows // KEY_PIECE)]
+    pieces.append(("router", 0, router_rows))
+
+    def far(kind, q, first, count):
+        buffer, size = (key_far, key_rows) if kind == "key" else (router_far, router_rows)
+        return buffer.at[pl.ds(pl.multiple_of(q * size + first, 16), count), :]
+
+    def forward(i, hop, q, axis):
+        block = far(pieces[i][0], q, *pieces[i][1:])
+        copy = remote(block, block, weight_send.at[hop, i], weight_recv.at[hop, i], partner(axis))
+        copy.start()
+        started.append(copy)
+        return copy
+
+    across = []
+    for i, (kind, first, count) in enumerate(pieces):
+        if kind == "key":
+            mine, weight, size, height = key_mine, key_weight, key_rows, half_rows
+        else:
+            mine, weight, size, height = router_mine, router_weight, router_rows, 4 * router_rows
+        for at, _, block_kind, col in blocks:
+            if block_kind != kind:
+                continue
+
+            def step(r, at=at, col=col):
+                r = pl.multiple_of(first + r, 16)
+                rows, cols = pl.ds(r, 16), slice(col, col + LANES)
+                gradient = full[pl.ds(pl.multiple_of(at + quarter * size + r, 16), 16), :]
+                new = adamw(
+                    mine[0, rows, cols],
+                    mine[1, rows, cols],
+                    mine[2, rows, cols],
+                    gradient.astype(F32),
+                    factor,
+                    0.1,
+                )[0]
+                weight[rows, cols] = new.astype(BF16)
+
+            rows_loop(count, 16, step)
+        copy = remote(
+            weight.at[pl.ds(first, count), :],
+            far(kind, quarter, first, count),
+            weight_send.at[0, i],
+            weight_recv.at[0, i],
+            partner("x"),
+        )
+        copy.start()
+        started.append(copy)
+        across.append(copy)
+
+    out_copies = []
+
+    def leave(source, target):
+        copy = pltpu.make_async_copy(source, target, out_sem.at[len(out_copies)])
+        copy.start()
+        out_copies.append(copy)
+
     for at, count, kind, col in blocks:
         target = key_out if kind == "key" else router_out
-
-        def place(r, at=at, col=col, target=target):
-            rows = pl.ds(pl.multiple_of(at + r, 16), 64)
-            target[pl.ds(r, 64), col : col + LANES] = full[rows, :]
-
-        rows_loop(count, 64, place)
-    for copy in started + gain_copies:
+        leave(full.at[pl.ds(at, count), :], target.at[:, pl.ds(col, LANES)])
+
+    beside, own, other = [], [], []
+    for i, copy in enumerate(across):
+        copy.wait_recv()
+        beside.append(forward(i, 1, quarter, 1))
+        own.append(forward(i, 2, quarter, 0))
+    neighbour = 2 * bit[0] + 1 - bit[1]
+    for i, copy in enumerate(beside):
+        copy.wait_recv()
+        other.append(forward(i, 3, neighbour, 0))
+    gain_copy.wait_recv()
+    gain_other[...] = gain_far[...]
+    for copy in own + other:
+        copy.wait_recv()
+    leave(key_far, key_other)
+    leave(router_far, router_other)
+    for copy in started + gain_copies + [gain_copy]:
         copy.wait_send()
-
-
-def reduce_grads(wide_size, key_grads, router_grads, gain_grads):
+    for copy in out_copies:
+        copy.wait()
+
+
+def update_kernel(
+    key_grad,
+    router_grad,
+    gain_grad,
+    factor_ref,
+    key_other,
+    router_other,
+    gain_other,
+    key_state,
+    router_state,
+    gain_state,
+    key_new,
+    router_new,
+    gain_new,
+    key_weight,
+    router_weight,
+    gain_weight,
+):
+    narrow = lax.axis_index("narrow")
+    factor = factor_ref[0:1, 0:1]
+
+    def update(state, grad, decay_rate, new):
+        values = adamw(
+            state[0][...], state[1][...], state[2][...], grad[...].astype(F32), factor, decay_rate
+        )
+        for ref, value in zip(new, values):
+            ref[...] = value
+        return values[0].astype(BF16)
+
+    key_weight[narrow] = update(key_state, key_grad, 0.1, key_new)
+    key_weight[1 - narrow] = key_other[...]
+
+    def columns(n, size):
+        return pl.ds(pl.multiple_of(n * size, 128), size)
+
+    size = router_other.shape[1]
+    router_weight[:, columns(narrow, size)] = update(router_state, router_grad, 0.1, router_new)
+    router_weight[:, columns(1 - narrow, size)] = router_other[...]
+    size = gain_other.shape[1]
+    gain_weight[:, columns(narrow, size)] = update(gain_state, gain_grad, 0.0, gain_new)
+    gain_weight[:, columns(1 - narrow, size)] = gain_other[...].astype(BF16)
+
+
+def update_all(sums, key_state, router_state, gain_state):
+    steps = 4
+    key_sum, router_sum, gain_sum, factor, key_other, router_other, gain_other = sums
+    (rows, width), (experts, cols), (_, gain) = key_sum.shape, router_sum.shape, gain_sum.shape
+    key_spec = pl.BlockSpec((rows // steps, width), lambda i: (i, 0))
+    router_spec = pl.BlockSpec((experts // steps, cols), lambda i: (i, 0))
+    gain_spec = pl.BlockSpec((1, gain), lambda i: (0, 0))
+    shape = jax.ShapeDtypeStruct
+    return pl.pallas_call(
+        update_kernel,
+        grid=(steps,),
+        out_shape=(
+            [shape((rows, width), F32)] * 3,
+            [shape((experts, cols), F32)] * 3,
+            [shape((1, gain), F32)] * 3,
+            shape((2, rows, width), BF16),
+            shape((experts, 2 * cols), BF16),
+            shape((1, 2 * gain), BF16),
+        ),
+        in_specs=[
+            key_spec,
+            router_spec,
+            gain_spec,
+            pl.BlockSpec((1, 128), lambda i: (0, 0)),
+            key_spec,
+            router_spec,
+            gain_spec,
+            [key_spec] * 3,
+            [router_spec] * 3,
+            [gain_spec] * 3,
+        ],
+        out_specs=(
+            [key_spec] * 3,
+            [router_spec] * 3,
+            [gain_spec] * 3,
+            pl.BlockSpec((2, rows // steps, width), lambda i: (0, i, 0)),
+            pl.BlockSpec((experts // steps, 2 * cols), lambda i: (i, 0)),
+            pl.BlockSpec((1, 2 * gain), lambda i: (0, 0)),
+        ),
+        compiler_params=pltpu.CompilerParams(vmem_limit_bytes=40 * 2**20),
+    )(
+        key_sum,
+        router_sum,
+        gain_sum,
+        factor,
+        key_other,
+        router_other,
+        gain_other,
+        key_state,
+        router_state,
+        gain_state,
+    )
+
+
+def reduce_grads(
+    wide_size, key_grads, router_grads, gain_grads, key_state, router_state, gain_state
+):
     key_shape, router_shape = key_grads.shape[3:], router_grads.shape[3:]
     gain_size = gain_grads.shape[3]
     blocks, total_rows = layout(key_shape, router_shape)
@@ -343,6 +569,10 @@
     stages = len(plans[0])
     count = math.prod(key_shape) + math.prod(router_shape) + gain_size
     vmem = pl.BlockSpec(memory_space=pltpu.VMEM)
+    hbm = pl.BlockSpec(memory_space=pl.ANY)
+    half_rows, width = key_shape[0] // 2, key_shape[1]
+    experts, half_cols = router_shape[0], router_shape[1] // 2
+    pieces = half_rows // 4 // KEY_PIECE + 1
     return pl.pallas_call(
         functools.partial(
             reduce_kernel, plans, blocks, total_rows, 0.5 * math.sqrt(count)
@@ -352,10 +582,15 @@
             jax.ShapeDtypeStruct((router_shape[0], router_shape[1] // 2), BF16),
             jax.ShapeDtypeStruct((1, gain_size // 2), F32),
             jax.ShapeDtypeStruct((1, 128), F32),
+            jax.ShapeDtypeStruct((half_rows, width), BF16),
+            jax.ShapeDtypeStruct((experts, half_cols), BF16),
+            jax.ShapeDtypeStruct((1, gain_size // 2), F32),
         ),
-        in_specs=[vmem] * 3,
-        out_specs=(vmem,) * 4,
+        in_specs=[hbm] * 3 + [[hbm] * 3] * 3,
+        out_specs=(hbm, hbm, vmem, vmem, hbm, hbm, vmem),
         scratch_shapes=[
+            pltpu.VMEM((2, 2, total_rows, LANES), BF16),
+            pltpu.VMEM((2, gain_size), BF16),
             pltpu.VMEM((2, total_rows, LANES), BF16),
             pltpu.VMEM((2, total_rows, LANES), F32),
             pltpu.VMEM((total_rows, LANES), BF16),
@@ -373,11 +608,26 @@
             pltpu.SemaphoreType.DMA((stages,)),
             pltpu.SemaphoreType.DMA((6,)),
             pltpu.SemaphoreType.DMA((6,)),
+            pltpu.VMEM((3, half_rows // 4, width), F32),
+            pltpu.VMEM((3, experts // 4, half_cols), F32),
+            pltpu.VMEM((3, 1, gain_size // 2), F32),
+            pltpu.VMEM((half_rows // 4, width), BF16),
+            pltpu.VMEM((experts // 4, half_cols), BF16),
+            pltpu.VMEM((half_rows, width), BF16),
+            pltpu.VMEM((experts, half_cols), BF16),
+            pltpu.VMEM((1, gain_size // 2), F32),
+            pltpu.VMEM((1, gain_size // 2), F32),
+            pltpu.SemaphoreType.DMA((2 * (len(blocks) + PARTS) + 1,)),
+            pltpu.SemaphoreType.DMA((9,)),
+            pltpu.SemaphoreType.DMA((4, pieces)),
+            pltpu.SemaphoreType.DMA((4, pieces)),
+            pltpu.SemaphoreType.DMA((2,)),
+            pltpu.SemaphoreType.DMA((len(blocks) + 2,)),
         ],
         compiler_params=pltpu.CompilerParams(
-            collective_id=0, has_side_effects=True, vmem_limit_bytes=40 * 2**20
+            collective_id=0, has_side_effects=True, vmem_limit_bytes=56 * 2**20
         ),
-    )(key_grads, router_grads, gain_grads)
+    )(key_grads, router_grads, gain_grads, key_state, router_state, gain_state)
 
 
 def on_device(
@@ -395,38 +645,22 @@
     gain_first,
     gain_second,
 ):
-    key_sum, router_sum, gain_sum, factor = reduce_grads(
-        wide_size, key_grads, router_grads, gain_grads
+    key_state = [key_master, key_first, key_second]
+    router_state = [router_master, router_first, router_second]
+    gain_state = [x.reshape(1, -1) for x in (gain_master, gain_first, gain_second)]
+    sums = reduce_grads(
+        wide_size, key_grads, router_grads, gain_grads, key_state, router_state, gain_state
     )
-    key_sum, router_sum = key_sum.astype(F32), router_sum.astype(F32)
-    gain_sum, factor = gain_sum[0], factor[0, 0]
-    key_new, key_first_new, key_second_new = adamw(
-        key_master, key_first, key_second, key_sum, factor, 0.1
-    )
-    router_new, router_first_new, router_second_new = adamw(
-        router_master, router_first, router_second, router_sum, factor, 0.1
-    )
-    gain_new, gain_first_new, gain_second_new = adamw(
-        gain_master, gain_first, gain_second, gain_sum, factor, 0.0
-    )
-    key_weight, router_weight, gain_weight = (
-        lax.all_gather(key_new.astype(BF16), "narrow", axis=0, tiled=True),
-        lax.all_gather(router_new.astype(BF16), "narrow", axis=1, tiled=True),
-        lax.all_gather(gain_new.astype(BF16), "narrow", axis=0, tiled=True),
+    key_new, router_new, gain_new, key_weight, router_weight, gain_weight = update_all(
+        sums, key_state, router_state, gain_state
     )
     return (
-        key_new,
-        key_first_new,
-        key_second_new,
-        router_new,
-        router_first_new,
-        router_second_new,
-        gain_new,
-        gain_first_new,
-        gain_second_new,
-        key_weight,
+        *key_new,
+        *router_new,
+        *[x.reshape(-1) for x in gain_new],
+        key_weight.reshape(-1, key_weight.shape[2]),
         router_weight,
-        gain_weight,
+        gain_weight.reshape(-1),
     )
 
 

time: 101 us -> 68.8 us (0.68)
  Pallas kernels: 40.9 us -> 60.8 us
  waiting for transfers between devices: 18.6 us -> 0 us
  between operations: 14.2 us -> 0.81 us
  blocking collectives: 11.1 us -> 0 us
  other arithmetic: 7.66 us -> 0.62 us
  local copies, waits for them, and re-layouts: 8.29 us -> 6.24 us
    all_gather x1 -> x0, waiting for transfers between devices: 18.5 us -> none  [on_device(): lax.all_gather(key_new.astype(BF16), 'narrow', axis=0, tiled=True)]
    pallas_call x1, Pallas kernels: 40.9 us -> 55.8 us  [reduce_grads(): pl.pallas_call(functools.partial(reduce_kernel, plans, blocks, total_rows...]
    all_gather x2 -> x0, blocking collectives: 11.1 us -> none  [the longest x1 6.71 us: on_device(): lax.all_gather(router_new.astype(BF16), 'narrow', axis=1, tiled=True)]
    convert_element_type x3 -> x0, other arithmetic: 7.62 us -> none  [the longest x1 5.95 us: on_device(): key_new.astype(BF16)]
    pallas_call x0 -> x1, Pallas kernels: none -> 5.09 us  [update_all(): pl.pallas_call(update_kernel, grid=(steps,), out_shape=([shape((rows, wid...]
    unnamed x25 -> x32, local copies, waits for them, and re-layouts: 8.29 us -> 6.24 us
  transfers between devices with their start and end apart: 1 -> 0, of which waited for: 1 -> 0; matrix products, arithmetic and copies ran while one was open for 2% -> 0% of each run, Pallas kernels for 0% -> 0%
where the time goes in v2:
time: 68.8 us; the launch traced here: 68.5 us
  Pallas kernels  60.8 us (88%)
  local copies, waits for them, and re-layouts  6.24 us (9%)
  between operations  0.81 us (1%)
    pallas_call x1, Pallas kernels, reduce_grads(): pl.pallas_call(functools.partial(reduce_kernel, plans, blocks, total_rows...  55.8 us
    unnamed x32, local copies, waits for them, and re-layouts  6.24 us
    pallas_call x1, Pallas kernels, update_all(): pl.pallas_call(update_kernel, grid=(steps,), out_shape=([shape((rows, wid...  5.09 us

profile of v2, /device:TPU:0, one launch (start us, length us, event | category | flops | bytes accessed | tf_op | source)
XLA Modules:
  0.0 68.5 jit_solution(5676088531021927155)
XLA Ops:
  0.6 0.0 copy-start
  0.7 0.0 copy-start.1
  0.7 0.0 copy-start.2
  0.7 0.0 copy-start.5
  0.7 0.0 copy-start.6
  0.7 0.0 copy-start.7
  0.7 0.0 copy-start.10
  0.7 0.0 copy-start.11
  0.7 0.0 copy-start.12
  0.7 55.8 %shard_map.211 = (bf16[1024,512]{1,0:T(8,128)(2,1)}, bf16[64,1024]{1,0:T(8,128)(2,1)}, f32[1,1024]{1,0:T(1,128)}, f32[1,128]{1,0:T(1,128)}, bf16[1024,512]{1,0:T...) custom-call(bf16[1,1,2,2048,512]{4,3,2,1,0:T(8,128)(2,1)} %key_ref.1, bf16[1,1,2,64,2048]{4,3,2,1,0:T(8,128)(2,1)} %router_ref.1, ...), custom_call_target="tpu_custom_call" | custom-call | tf_op jit(solution)/shard_map/pallas_call | solution.py:576
  56.5 0.0 copy-done
  56.5 0.0 copy-done.1
  56.5 0.0 copy-done.2
  56.5 0.0 copy-done.5
  56.5 0.0 copy-done.6
  56.6 0.0 copy-done.7
  56.6 0.0 copy-done.10
  56.6 0.0 copy-done.11
  56.6 0.0 copy-done.12
  56.6 0.0 copy-start.3
  56.6 1.2 %copy-done.3 = bf16[1024,512]{1,0:T(8,128)(2,1)S(1)} copy-done((bf16[1024,512]{1,0:T(8,128)(2,1)S(1)}, bf16[1024,512]{1,0:T(8,128)(2,1)}, u32[]{:S(2)}) %copy-start.3) | copy-done | bytes 1048600
  57.8 0.0 copy-start.4
  57.8 1.2 %copy-done.4 = bf16[1024,512]{1,0:T(8,128)(2,1)S(1)} copy-done((bf16[1024,512]{1,0:T(8,128)(2,1)S(1)}, bf16[1024,512]{1,0:T(8,128)(2,1)}, u32[]{:S(2)}) %copy-start.4) | copy-done | bytes 1048600
  59.0 0.0 copy-start.8
  59.0 0.9 %copy-done.8 = bf16[64,1024]{1,0:T(8,128)(2,1)S(1)} copy-done((bf16[64,1024]{1,0:T(8,128)(2,1)S(1)}, bf16[64,1024]{1,0:T(8,128)(2,1)}, u32[]{:S(2)}) %copy-start.8) | copy-done | bytes 131096
  60.0 0.0 copy-start.9
  60.0 0.9 %copy-done.9 = bf16[64,1024]{1,0:T(8,128)(2,1)S(1)} copy-done((bf16[64,1024]{1,0:T(8,128)(2,1)S(1)}, bf16[64,1024]{1,0:T(8,128)(2,1)}, u32[]{:S(2)}) %copy-start.9) | copy-done | bytes 131096
  60.9 0.0 copy-start.13
  60.9 0.7 copy-done.13
  61.5 0.0 copy-start.14
  61.5 0.7 copy-done.14
  62.2 0.0 copy-start.15
  62.2 0.6 copy-done.15
  62.8 5.1 %shard_map.212 = (f32[1024,512]{1,0:T(8,128)}, f32[1024,512]{1,0:T(8,128)}, f32[1024,512]{1,0:T(8,128)}, f32[64,1024]{1,0:T(8,128)}, f32[64,1024]{1,0:T(8,128)},...) custom-call(bf16[1024,512]{1,0:T(8,128)(2,1)S(1)} %copy-done.3, ...), custom_call_target="tpu_custom_call" | custom-call | tf_op jit(solution)/shard_map/pallas_call | solution.py:515
  67.9 0.6 reduce
Async XLA Ops:
  0.6 55.9 %copy-start = (f32[1024,512]{1,0:T(8,128)S(1)}, f32[1024,512]{1,0:T(8,128)}, u32[]{:S(2)}) copy-start(f32[1024,512]{1,0:T(8,128)} %key_state_0_.3) | copy-start | bytes 6291460
  0.7 55.9 %copy-start.1 = (f32[1024,512]{1,0:T(8,128)S(1)}, f32[1024,512]{1,0:T(8,128)}, u32[]{:S(2)}) copy-start(f32[1024,512]{1,0:T(8,128)} %key_state_1_.3) | copy-start | bytes 6291460
  0.7 55.9 %copy-start.2 = (f32[1024,512]{1,0:T(8,128)S(1)}, f32[1024,512]{1,0:T(8,128)}, u32[]{:S(2)}) copy-start(f32[1024,512]{1,0:T(8,128)} %key_state_2_.3) | copy-start | bytes 6291460
  0.7 55.9 %copy-start.5 = (f32[64,1024]{1,0:T(8,128)S(1)}, f32[64,1024]{1,0:T(8,128)}, u32[]{:S(2)}) copy-start(f32[64,1024]{1,0:T(8,128)} %router_state_0_.3) | copy-start | bytes 786436
  0.7 55.9 %copy-start.6 = (f32[64,1024]{1,0:T(8,128)S(1)}, f32[64,1024]{1,0:T(8,128)}, u32[]{:S(2)}) copy-start(f32[64,1024]{1,0:T(8,128)} %router_state_1_.3) | copy-start | bytes 786436
  0.7 55.9 %copy-start.7 = (f32[64,1024]{1,0:T(8,128)S(1)}, f32[64,1024]{1,0:T(8,128)}, u32[]{:S(2)}) copy-start(f32[64,1024]{1,0:T(8,128)} %router_state_2_.3) | copy-start | bytes 786436
  0.7 55.9 %copy-start.10 = (f32[1024]{0:T(1024)S(1)}, f32[1024]{0:T(1024)}, u32[]{:S(2)}) copy-start(f32[1024]{0:T(1024)} %param.21) | copy-start | bytes 12292
  0.7 55.9 %copy-start.11 = (f32[1024]{0:T(1024)S(1)}, f32[1024]{0:T(1024)}, u32[]{:S(2)}) copy-start(f32[1024]{0:T(1024)} %param.22) | copy-start | bytes 12292
  0.7 55.9 %copy-start.12 = (f32[1024]{0:T(1024)S(1)}, f32[1024]{0:T(1024)}, u32[]{:S(2)}) copy-start(f32[1024]{0:T(1024)} %param.23) | copy-start | bytes 12292
  56.6 1.2 %copy-start.3 = (bf16[1024,512]{1,0:T(8,128)(2,1)S(1)}, bf16[1024,512]{1,0:T(8,128)(2,1)}, u32[]{:S(2)}) copy-start(bf16[1024,512]{1,0:T(8,128)(2,1)} %get-tuple-element.31.key_grad) | copy-start | bytes 3145732
  57.8 1.2 %copy-start.4 = (bf16[1024,512]{1,0:T(8,128)(2,1)S(1)}, bf16[1024,512]{1,0:T(8,128)(2,1)}, u32[]{:S(2)}) copy-start(bf16[1024,512]{1,0:T(8,128)(2,1)} %get-tuple-element.35.key_other) | copy-start | bytes 3145732
  59.0 0.9 %copy-start.8 = (bf16[64,1024]{1,0:T(8,128)(2,1)S(1)}, bf16[64,1024]{1,0:T(8,128)(2,1)}, u32[]{:S(2)}) copy-start(bf16[64,1024]{1,0:T(8,128)(2,1)} %get-tuple-element.32.router_grad) | copy-start | bytes 393220
  60.0 0.9 %copy-start.9 = (bf16[64,1024]{1,0:T(8,128)(2,1)S(1)}, bf16[64,1024]{1,0:T(8,128)(2,1)}, u32[]{:S(2)}) copy-start(bf16[64,1024]{1,0:T(8,128)(2,1)} %get-tuple-element.36.router_other) | copy-start | bytes 393220
  60.9 0.7 copy-start.13
  61.5 0.7 copy-start.14
  62.2 0.6 copy-start.15

commit v3 on v2

--- a/solution.py
+++ b/solution.py
@@ -15,8 +15,8 @@
 bias_one = 1.0 - 0.9**10
 bias_two = 1.0 - 0.95**10
 
-LANES = 256
-PARTS = 3
+LANES = 128
+PARTS = 6
 HALVED_BITS = 4
 KEY_PIECE = 64
 F32, BF16 = jnp.float32, jnp.bfloat16
@@ -54,7 +54,7 @@
 
 
 def part_orders():
-    return (("x", 1, 2), (1, 2, "x"), (2, "x", 1))
+    return (("x", 1, 2), (1, 2, "x"), (2, "x", 1)) * (PARTS // 3)
 
 
 def stage_shapes(part_rows, wide_bits):
@@ -137,6 +137,11 @@
             return (wide, 1 - narrow)
         return (wide + (1 - 2 * bit[axis]) * 2**axis, narrow)
 
+    diagonal = (partner(3)[0], 1 - narrow)
+    friends = [partner(a) for a in ["x"] + list(range(wide_bits))] + [diagonal]
+    barrier = pltpu.get_barrier_semaphore()
+    for friend in friends:
+        pl.semaphore_signal(barrier, inc=1, device_id=friend, device_id_type=pl.DeviceIdType.MESH)
     half_rows, half_cols = key_ref.shape[3] // 2, router_ref.shape[4] // 2
     gain_load = pltpu.make_async_copy(gain_ref.at[0, 0], gain_grads, load_sem.at[0])
     gain_load.start()
@@ -173,11 +178,6 @@
         copy.start()
         mine_loads.append(copy)
 
-    diagonal = (partner(3)[0], 1 - narrow)
-    friends = [partner(a) for a in ["x"] + list(range(wide_bits))] + [diagonal]
-    barrier = pltpu.get_barrier_semaphore()
-    for friend in friends:
-        pl.semaphore_signal(barrier, inc=1, device_id=friend, device_id_type=pl.DeviceIdType.MESH)
     pl.semaphore_wait(barrier, len(friends))
 
     def remote(src, dst, send, recv, to):
@@ -217,12 +217,11 @@
         kept = pl.multiple_of(p * part_rows + bit[0] * count, 16)
 
         def fill(r, first):
-            rows = pl.ds(pl.multiple_of(first + r, 16), 48)
+            rows = pl.ds(pl.multiple_of(first + r, 16), 96)
             for half in range(2):
-                one, two = grads[0, half, rows, :], grads[1, half, rows, :]
-                local[half, rows, :] = (one.astype(F32) + two.astype(F32)).astype(BF16)
-
-        rows_loop(count, 48, functools.partial(fill, first=sent))
+                local[half, rows, :] = grads[0, half, rows, :] + grads[1, half, rows, :]
+
+        rows_loop(count, 96, functools.partial(fill, first=sent))
         copy = remote(
             local.at[:, pl.ds(sent, count), :],
             recv_bufs[p][0],
@@ -233,7 +232,7 @@
         copy.start()
         copies.append(copy)
         started.append(copy)
-        rows_loop(count, 48, functools.partial(fill, first=kept))
+        rows_loop(count, 96, functools.partial(fill, first=kept))
 
     base = [pl.multiple_of(p * part_rows + bit[0] * (part_rows // 2), 16) for p in range(PARTS)]
     rows_now = [part_rows // 2] * PARTS
@@ -255,7 +254,7 @@
             copies[p].wait_recv()
             halves = [(narrow, 0)] if split[p] else [(0, 0), (1, 1)]
             send_buf = send_bufs[p][stage - 1]
-            step = 48
+            step = min(96, shape[1])
             if axis == "x":
                 send_sets, keep_sets = [(1 - narrow, 1 - narrow, 0)], [(narrow, narrow)]
                 send_offset = keep_offset = 0
@@ -396,28 +395,18 @@
     across = []
     for i, (kind, first, count) in enumerate(pieces):
         if kind == "key":
-            mine, weight, size, height = key_mine, key_weight, key_rows, half_rows
+            mine, weight, size = key_mine, key_weight, key_rows
         else:
-            mine, weight, size, height = router_mine, router_weight, router_rows, 4 * router_rows
+            mine, weight, size = router_mine, router_weight, router_rows
         for at, _, block_kind, col in blocks:
             if block_kind != kind:
                 continue
 
-            def step(r, at=at, col=col):
-                r = pl.multiple_of(first + r, 16)
-                rows, cols = pl.ds(r, 16), slice(col, col + LANES)
-                gradient = full[pl.ds(pl.multiple_of(at + quarter * size + r, 16), 16), :]
-                new = adamw(
-                    mine[0, rows, cols],
-                    mine[1, rows, cols],
-                    mine[2, rows, cols],
-                    gradient.astype(F32),
-                    factor,
-                    0.1,
-                )[0]
-                weight[rows, cols] = new.astype(BF16)
-
-            rows_loop(count, 16, step)
+            rows, cols = slice(first, first + count), slice(col, col + LANES)
+            start = pl.multiple_of(at + quarter * size + first, 16)
+            gradient = full[pl.ds(start, count), :].astype(F32)
+            state = [mine[j, rows, cols] for j in range(3)]
+            weight[rows, cols] = adamw(*state, gradient, factor, 0.1)[0].astype(BF16)
         copy = remote(
             weight.at[pl.ds(first, count), :],
             far(kind, quarter, first, count),
@@ -482,25 +471,32 @@
     narrow = lax.axis_index("narrow")
     factor = factor_ref[0:1, 0:1]
 
-    def update(state, grad, decay_rate, new):
-        values = adamw(
-            state[0][...], state[1][...], state[2][...], grad[...].astype(F32), factor, decay_rate
-        )
+    def update(state, grad, decay_rate, new, rows):
+        old = [ref[rows, :] for ref in state]
+        values = adamw(*old, grad[rows, :].astype(F32), factor, decay_rate)
         for ref, value in zip(new, values):
-            ref[...] = value
+            ref[rows, :] = value
         return values[0].astype(BF16)
 
-    key_weight[narrow] = update(key_state, key_grad, 0.1, key_new)
-    key_weight[1 - narrow] = key_other[...]
+    def key_step(r):
+        rows = pl.ds(r, 32)
+        key_weight[narrow, rows, :] = update(key_state, key_grad, 0.1, key_new, rows)
+        key_weight[1 - narrow, rows, :] = key_other[rows, :]
+
+    rows_loop(key_grad.shape[0], 32, key_step)
 
     def columns(n, size):
         return pl.ds(pl.multiple_of(n * size, 128), size)
 
     size = router_other.shape[1]
-    router_weight[:, columns(narrow, size)] = update(router_state, router_grad, 0.1, router_new)
+    router_weight[:, columns(narrow, size)] = update(
+        router_state, router_grad, 0.1, router_new, slice(None)
+    )
     router_weight[:, columns(1 - narrow, size)] = router_other[...]
     size = gain_other.shape[1]
-    gain_weight[:, columns(narrow, size)] = update(gain_state, gain_grad, 0.0, gain_new)
+    gain_weight[:, columns(narrow, size)] = update(
+        gain_state, gain_grad, 0.0, gain_new, slice(None)
+    )
     gain_weight[:, columns(1 - narrow, size)] = gain_other[...].astype(BF16)
 
 
@@ -543,7 +539,7 @@
             pl.BlockSpec((experts // steps, 2 * cols), lambda i: (i, 0)),
             pl.BlockSpec((1, 2 * gain), lambda i: (0, 0)),
         ),
-        compiler_params=pltpu.CompilerParams(vmem_limit_bytes=40 * 2**20),
+        compiler_params=pltpu.CompilerParams(vmem_limit_bytes=62 * 2**20),
     )(
         key_sum,
         router_sum,

time: 68.8 us -> 64.3 us (0.935)
  local copies, waits for them, and re-layouts: 6.24 us -> 0 us
  Pallas kernels: 60.8 us -> 62.1 us
  other arithmetic: 0.62 us -> 1.32 us
    unnamed x32 -> x0, local copies, waits for them, and re-layouts: 6.24 us -> none
    pallas_call x1, Pallas kernels: 5.09 us -> 9.57 us  [update_all(): pl.pallas_call(update_kernel, grid=(steps,), out_shape=([shape((rows, wid...]
    pallas_call x1, Pallas kernels: 55.8 us -> 52.5 us  [reduce_grads(): pl.pallas_call(functools.partial(reduce_kernel, plans, blocks, total_rows...]
    pallas_call x1, other arithmetic: 0.62 us -> 1.32 us  [update_all(): pl.pallas_call(update_kernel, grid=(steps,), out_shape=([shape((rows, wid...]
where the time goes in v3:
time: 64.3 us; the launch traced here: 64 us
  Pallas kernels  62.1 us (97%)
  other arithmetic  1.32 us (2%)
  between operations  0.66 us (1%)
    pallas_call x1, Pallas kernels, reduce_grads(): pl.pallas_call(functools.partial(reduce_kernel, plans, blocks, total_rows...  52.5 us
    pallas_call x1, Pallas kernels, update_all(): pl.pallas_call(update_kernel, grid=(steps,), out_shape=([shape((rows, wid...  9.57 us
    pallas_call x1, other arithmetic, update_all(): pl.pallas_call(update_kernel, grid=(steps,), out_shape=([shape((rows, wid...  1.32 us

profile of v3, /device:TPU:0, one launch (start us, length us, event | category | flops | bytes accessed | tf_op | source)
XLA Modules:
  0.0 64.0 jit_solution(4447971828507171109)
XLA Ops:
  0.6 52.5 %shard_map.211 = (bf16[1024,512]{1,0:T(8,128)(2,1)}, bf16[64,1024]{1,0:T(8,128)(2,1)}, f32[1,1024]{1,0:T(1,128)}, f32[1,128]{1,0:T(1,128)}, bf16[1024,512]{1,0:T...) custom-call(bf16[1,1,2,2048,512]{4,3,2,1,0:T(8,128)(2,1)} %key_ref.1, bf16[1,1,2,64,2048]{4,3,2,1,0:T(8,128)(2,1)} %router_ref.1, ...), custom_call_target="tpu_custom_call" | custom-call | tf_op jit(solution)/shard_map/pallas_call | solution.py:572
  53.2 9.6 %shard_map.212 = (f32[1024,512]{1,0:T(8,128)}, f32[1024,512]{1,0:T(8,128)}, f32[1024,512]{1,0:T(8,128)}, f32[64,1024]{1,0:T(8,128)}, f32[64,1024]{1,0:T(8,128)},...) custom-call(bf16[1024,512]{1,0:T(8,128)(2,1)} %get-tuple-element.31., ...), custom_call_target="tpu_custom_call" | custom-call | tf_op jit(solution)/shard_map/pallas_call | solution.py:511
  62.7 1.3 %reduce = bf16[2048]{0:T(1024)(128)(2,1)} reduce(bf16[1,2048]{1,0:T(2,128)(2,1)} %get-tuple-element.49, bf16[]{:T(256)} %constant.3), dimensions={0}, to_apply=%get-tuple-element.49.reduce_sub_computation | reduce | bytes 8194 | tf_op jit(solution)/shard_map/pallas_call | solution.py:511

commit v4 on v3

--- a/solution.py
+++ b/solution.py
@@ -18,7 +18,6 @@
 LANES = 128
 PARTS = 6
 HALVED_BITS = 4
-KEY_PIECE = 64
 F32, BF16 = jnp.float32, jnp.bfloat16
 
 
@@ -84,13 +83,8 @@
     key_state,
     router_state,
     gain_state,
-    key_out,
-    router_out,
-    gain_out,
-    factor_out,
-    key_other,
-    router_other,
-    gain_other,
+    packed_out,
+    small_out,
     grads,
     gain_grads,
     local,
@@ -110,17 +104,16 @@
     gain_recv,
     square_send,
     square_recv,
-    key_mine,
-    router_mine,
+    state,
     gain_mine,
-    key_weight,
-    router_weight,
-    key_far,
-    router_far,
+    weight,
+    far,
+    gain_own,
     gain_new,
     gain_far,
+    small,
     load_sem,
-    mine_sem,
+    state_sem,
     weight_send,
     weight_recv,
     gain_far_sem,
@@ -165,19 +158,6 @@
                 part_loads.append(copy)
         loads.append(part_loads)
 
-    quarter = 2 * bit[0] + bit[1]
-    key_rows, router_rows = half_rows // 4, router_ref.shape[3] // 4
-    mine_loads = []
-    for i, (state, mine, count) in enumerate(
-        [(r, key_mine, key_rows) for r in key_state]
-        + [(r, router_mine, router_rows) for r in router_state]
-        + [(r, gain_mine, 1) for r in gain_state]
-    ):
-        rows = pl.ds(pl.multiple_of(quarter * count, 16), count) if count > 1 else pl.ds(0, 1)
-        copy = pltpu.make_async_copy(state.at[rows, :], mine.at[i % 3], mine_sem.at[i])
-        copy.start()
-        mine_loads.append(copy)
-
     pl.semaphore_wait(barrier, len(friends))
 
     def remote(src, dst, send, recv, to):
@@ -233,6 +213,19 @@
         copies.append(copy)
         started.append(copy)
         rows_loop(count, 96, functools.partial(fill, first=kept))
+
+    state_loads = []
+
+    def load_state(source, target):
+        copy = pltpu.make_async_copy(source, target, state_sem.at[len(state_loads)])
+        copy.start()
+        state_loads.append(copy)
+
+    for i in range(3):
+        load_state(gain_state[i], gain_mine.at[i])
+        for at, count, kind, col in blocks:
+            source = key_state[i] if kind == "key" else router_state[i]
+            load_state(source.at[:, pl.ds(col, LANES)], state.at[i, pl.ds(at, count), :])
 
     base = [pl.multiple_of(p * part_rows + bit[0] * (part_rows // 2), 16) for p in range(PARTS)]
     rows_now = [part_rows // 2] * PARTS
@@ -352,71 +345,77 @@
     gain_copies[stages - 1].wait_recv()
     gain_sum = gain_val[stages - 1] + gain_in[stages - 1]
     gain_val[stages] = gain_sum
-    left = pl.multiple_of(narrow * gain_out.shape[1], 128)
-    gain_out[...] = gain_val[stages, :, pl.ds(left, gain_out.shape[1])]
+    left = pl.multiple_of(narrow * gain_own.shape[1], 128)
+    gain_own[...] = gain_val[stages, :, pl.ds(left, gain_own.shape[1])]
     for copy in square_copies:
         copy.wait_recv()
     square_val[1] = (square_val[0] + square_in[0]) + (square_in[1] + square_in[2])
-    for stage in range(1, 4):
-        square_copy = send_square(stage, stage + 2, partner((2, 1, 0)[stage - 1]))
-        for p in range(PARTS):
-            gathers[p].wait_recv()
-            gathers[p] = gather(p, stage)
+    square_copy = send_square(1, 3, partner(2))
+    for p in range(PARTS):
+        gathers[p].wait_recv()
+        gathers[p] = gather(p, 1)
+    for stage in range(2, 4):
         square_copy.wait_recv()
-        square_val[stage + 1] = square_val[stage] + square_in[stage + 2]
-    total = jnp.sum(square_val[4]) + jnp.sum(gain_sum * gain_sum)
-    total = jnp.full(factor_out.shape, total, F32)
-    factor_out[...] = clip_limit / jnp.maximum(jnp.sqrt(total), clip_limit)
-    for copy in gathers:
-        copy.wait_recv()
-    for copy in mine_loads:
+        square_val[stage] = square_val[stage - 1] + square_in[stage + 1]
+        square_copy = send_square(stage, stage + 2, partner((1, 0)[stage - 2]))
+    for copy in state_loads:
         copy.wait()
-
-    factor = factor_out[0:1, 0:1]
+    square_copy.wait_recv()
+    total = jnp.sum(square_val[3] + square_in[5]) + jnp.sum(gain_sum * gain_sum)
+    total = jnp.full((8, 128), total, F32)
+    gain_tiles = gain_own.shape[1] // 128
+    small[2 * gain_tiles :, :] = clip_limit / jnp.maximum(jnp.sqrt(total), clip_limit)
+    factor = small[2 * gain_tiles : 2 * gain_tiles + 1, 0:1]
+
+    def forward(p, hop, start, axis):
+        block = far.at[pl.ds(start, quarter_rows), :]
+        copy = remote(block, block, weight_send.at[hop, p], weight_recv.at[hop, p], partner(axis))
+        copy.start()
+        started.append(copy)
+        return copy
+
+    quarter_rows = part_rows // 4
+    held, across = [], []
+    for p in range(PARTS):
+        gathers[p].wait_recv()
+        start = base[p]
+        held.append(start)
+        gathers[p] = gather(p, 2)
+
+        def renew(r, p=p, start=start):
+            rows = pl.ds(pl.multiple_of(start + r, 16), 64)
+            old = [state[i, rows, :] for i in range(3)]
+            new = adamw(*old, full[rows, :].astype(F32), factor, 0.1)[0]
+            weight[p, pl.ds(r, 64), :] = new.astype(BF16)
+
+        rows_loop(quarter_rows, 64, renew)
+        copy = remote(
+            weight.at[p],
+            far.at[pl.ds(start, quarter_rows), :],
+            weight_send.at[0, p],
+            weight_recv.at[0, p],
+            partner("x"),
+        )
+        copy.start()
+        started.append(copy)
+        across.append(copy)
     gain_new[...] = adamw(
-        gain_mine[0], gain_mine[1], gain_mine[2], gain_out[...], factor, 0.0
+        gain_mine[0], gain_mine[1], gain_mine[2], gain_own[...], factor, 0.0
     )[0]
     gain_copy = remote(gain_new, gain_far, gain_far_sem.at[0], gain_far_sem.at[1], partner("x"))
     gain_copy.start()
-    pieces = [("key", i * KEY_PIECE, KEY_PIECE) for i in range(key_rows // KEY_PIECE)]
-    pieces.append(("router", 0, router_rows))
-
-    def far(kind, q, first, count):
-        buffer, size = (key_far, key_rows) if kind == "key" else (router_far, router_rows)
-        return buffer.at[pl.ds(pl.multiple_of(q * size + first, 16), count), :]
-
-    def forward(i, hop, q, axis):
-        block = far(pieces[i][0], q, *pieces[i][1:])
-        copy = remote(block, block, weight_send.at[hop, i], weight_recv.at[hop, i], partner(axis))
-        copy.start()
-        started.append(copy)
-        return copy
-
-    across = []
-    for i, (kind, first, count) in enumerate(pieces):
-        if kind == "key":
-            mine, weight, size = key_mine, key_weight, key_rows
-        else:
-            mine, weight, size = router_mine, router_weight, router_rows
-        for at, _, block_kind, col in blocks:
-            if block_kind != kind:
-                continue
-
-            rows, cols = slice(first, first + count), slice(col, col + LANES)
-            start = pl.multiple_of(at + quarter * size + first, 16)
-            gradient = full[pl.ds(start, count), :].astype(F32)
-            state = [mine[j, rows, cols] for j in range(3)]
-            weight[rows, cols] = adamw(*state, gradient, factor, 0.1)[0].astype(BF16)
-        copy = remote(
-            weight.at[pl.ds(first, count), :],
-            far(kind, quarter, first, count),
-            weight_send.at[0, i],
-            weight_recv.at[0, i],
-            partner("x"),
-        )
-        copy.start()
-        started.append(copy)
-        across.append(copy)
+
+    beside, own, other = [], [], []
+    for p in range(PARTS):
+        gathers[p].wait_recv()
+        gathers[p] = gather(p, 3)
+        across[p].wait_recv()
+        beside.append(forward(p, 1, held[p], gather_axes[p][2]))
+        own.append(forward(p, 2, held[p], 0))
+    for p in range(PARTS):
+        beside[p].wait_recv()
+        step = (1 - 2 * bit[gather_axes[p][2]]) * quarter_rows
+        other.append(forward(p, 3, pl.multiple_of(held[p] + step, 16), 0))
 
     out_copies = []
 
@@ -425,25 +424,28 @@
         copy.start()
         out_copies.append(copy)
 
-    for at, count, kind, col in blocks:
-        target = key_out if kind == "key" else router_out
-        leave(full.at[pl.ds(at, count), :], target.at[:, pl.ds(col, LANES)])
-
-    beside, own, other = [], [], []
-    for i, copy in enumerate(across):
+    def leave_packed(source, place):
+        keys = [at for at, _, kind, _ in blocks if kind == "key"]
+        for i, at in enumerate(keys):
+            leave(source.at[pl.ds(at, half_rows), :], packed_out.at[place, i])
+        at = len(keys) * half_rows
+        rest = total_rows - at
+        leave(
+            source.at[pl.ds(at, rest), :], packed_out.at[place, len(keys), pl.ds(0, rest), :]
+        )
+
+    for copy in gathers:
         copy.wait_recv()
-        beside.append(forward(i, 1, quarter, 1))
-        own.append(forward(i, 2, quarter, 0))
-    neighbour = 2 * bit[0] + 1 - bit[1]
-    for i, copy in enumerate(beside):
-        copy.wait_recv()
-        other.append(forward(i, 3, neighbour, 0))
+    leave_packed(full, 0)
     gain_copy.wait_recv()
-    gain_other[...] = gain_far[...]
+    for j in range(gain_tiles):
+        cols = slice(128 * j, 128 * (j + 1))
+        small[j : j + 1, :] = gain_own[:, cols]
+        small[gain_tiles + j : gain_tiles + j + 1, :] = gain_far[:, cols]
+    leave(small, small_out.at[pl.ds(0, small.shape[0]), :])
     for copy in own + other:
         copy.wait_recv()
-    leave(key_far, key_other)
-    leave(router_far, router_other)
+    leave_packed(far, 1)
     for copy in started + gain_copies + [gain_copy]:
         copy.wait_send()
     for copy in out_copies:
@@ -451,13 +453,8 @@
 
 
 def update_kernel(
-    key_grad,
-    router_grad,
-    gain_grad,
-    factor_ref,
-    key_other,
-    router_other,
-    gain_other,
+    packed,
+    small_in,
     key_state,
     router_state,
     gain_state,
@@ -467,45 +464,89 @@
     key_weight,
     router_weight,
     gain_weight,
+    keys,
+    routers,
+    small,
+    gain_rows,
+    key_sem,
+    other_sem,
 ):
-    narrow = lax.axis_index("narrow")
-    factor = factor_ref[0:1, 0:1]
-
-    def update(state, grad, decay_rate, new, rows):
-        old = [ref[rows, :] for ref in state]
-        values = adamw(*old, grad[rows, :].astype(F32), factor, decay_rate)
+    narrow, at = lax.axis_index("narrow"), pl.program_id(0)
+    steps = pl.num_programs(0)
+    blocks, block_rows, experts = keys.shape[1], key_new[0].shape[0], router_new[0].shape[0]
+    gain_tiles = gain_rows.shape[0] // 2
+
+    def key_copy(i):
+        rows = pl.ds(pl.multiple_of(i * block_rows, 16), block_rows)
+        return pltpu.make_async_copy(
+            packed.at[:, pl.ds(0, blocks), rows, :], keys.at[:, :, rows, :], key_sem.at[i]
+        )
+
+    other_copies = [
+        pltpu.make_async_copy(
+            small_in.at[pl.ds(0, small.shape[0]), :], small, other_sem.at[0]
+        ),
+        pltpu.make_async_copy(
+            packed.at[:, blocks, pl.ds(0, routers.shape[1]), :], routers, other_sem.at[1]
+        ),
+    ]
+
+    @pl.when(at == 0)
+    def _():
+        for copy in other_copies:
+            copy.start()
+        for i in range(keys.shape[2] // block_rows):
+            key_copy(i).start()
+        for copy in other_copies:
+            copy.wait()
+
+    factor = small[2 * gain_tiles : 2 * gain_tiles + 1, 0:1]
+
+    def update(state, gradient, decay_rate, new, rows, cols):
+        old = [ref[rows, cols] for ref in state]
+        values = adamw(*old, gradient.astype(F32), factor, decay_rate)
         for ref, value in zip(new, values):
-            ref[rows, :] = value
-        return values[0].astype(BF16)
-
-    def key_step(r):
-        rows = pl.ds(r, 32)
-        key_weight[narrow, rows, :] = update(key_state, key_grad, 0.1, key_new, rows)
-        key_weight[1 - narrow, rows, :] = key_other[rows, :]
-
-    rows_loop(key_grad.shape[0], 32, key_step)
-
-    def columns(n, size):
-        return pl.ds(pl.multiple_of(n * size, 128), size)
-
-    size = router_other.shape[1]
-    router_weight[:, columns(narrow, size)] = update(
-        router_state, router_grad, 0.1, router_new, slice(None)
+            ref[rows, cols] = value
+        return values[0]
+
+    @pl.when(at == 0)
+    def _():
+        for j in range(gain_tiles):
+            cols = slice(128 * j, 128 * (j + 1))
+            value = update(
+                gain_state, small[j : j + 1, :], 0.0, gain_new, slice(0, 1), cols
+            )
+            gain_rows[pl.ds(narrow * gain_tiles + j, 1), :] = value
+            other = small[gain_tiles + j : gain_tiles + j + 1, :]
+            gain_rows[pl.ds((1 - narrow) * gain_tiles + j, 1), :] = other
+        gain_weight[...] = gain_rows[...].astype(BF16)
+
+    rows = pl.ds(pl.multiple_of(at * experts, 16), experts)
+    value = update(
+        router_state, routers[0, rows, :], 0.1, router_new, slice(None), slice(None)
     )
-    router_weight[:, columns(1 - narrow, size)] = router_other[...]
-    size = gain_other.shape[1]
-    gain_weight[:, columns(narrow, size)] = update(
-        gain_state, gain_grad, 0.0, gain_new, slice(None)
-    )
-    gain_weight[:, columns(1 - narrow, size)] = gain_other[...].astype(BF16)
-
-
-def update_all(sums, key_state, router_state, gain_state):
-    steps = 4
-    key_sum, router_sum, gain_sum, factor, key_other, router_other, gain_other = sums
-    (rows, width), (experts, cols), (_, gain) = key_sum.shape, router_sum.shape, gain_sum.shape
+
+    def columns(n):
+        return pl.ds(pl.multiple_of((n * steps + at) * LANES, 128), LANES)
+
+    router_weight[:, columns(narrow)] = value.astype(BF16)
+    router_weight[:, columns(1 - narrow)] = routers[1, rows, :]
+
+    key_copy(at).wait()
+    rows = pl.ds(pl.multiple_of(at * block_rows, 16), block_rows)
+    for j in range(blocks):
+        cols = slice(LANES * j, LANES * (j + 1))
+        value = update(key_state, keys[0, j, rows, :], 0.1, key_new, slice(None), cols)
+        key_weight[narrow, :, cols] = value.astype(BF16)
+        key_weight[1 - narrow, :, cols] = keys[1, j, rows, :]
+
+
+def update_all(packed, small, key_state, router_state, gain_state):
+    (rows, width), (experts, cols) = key_state[0].shape, router_state[0].shape
+    gain = gain_state[0].shape[1]
+    steps = cols // LANES
     key_spec = pl.BlockSpec((rows // steps, width), lambda i: (i, 0))
-    router_spec = pl.BlockSpec((experts // steps, cols), lambda i: (i, 0))
+    router_spec = pl.BlockSpec((experts, LANES), lambda i: (0, i))
     gain_spec = pl.BlockSpec((1, gain), lambda i: (0, 0))
     shape = jax.ShapeDtypeStruct
     return pl.pallas_call(
@@ -517,41 +558,28 @@
             [shape((1, gain), F32)] * 3,
             shape((2, rows, width), BF16),
             shape((experts, 2 * cols), BF16),
-            shape((1, 2 * gain), BF16),
+            shape((2 * gain // 128, 128), BF16),
         ),
-        in_specs=[
-            key_spec,
-            router_spec,
-            gain_spec,
-            pl.BlockSpec((1, 128), lambda i: (0, 0)),
-            key_spec,
-            router_spec,
-            gain_spec,
-            [key_spec] * 3,
-            [router_spec] * 3,
-            [gain_spec] * 3,
-        ],
+        in_specs=[pl.BlockSpec(memory_space=pltpu.HBM)] * 2
+        + [[key_spec] * 3, [router_spec] * 3, [gain_spec] * 3],
         out_specs=(
             [key_spec] * 3,
             [router_spec] * 3,
             [gain_spec] * 3,
             pl.BlockSpec((2, rows // steps, width), lambda i: (0, i, 0)),
-            pl.BlockSpec((experts // steps, 2 * cols), lambda i: (i, 0)),
-            pl.BlockSpec((1, 2 * gain), lambda i: (0, 0)),
+            pl.BlockSpec((experts, 2 * cols), lambda i: (0, 0)),
+            pl.BlockSpec((2 * gain // 128, 128), lambda i: (0, 0)),
         ),
-        compiler_params=pltpu.CompilerParams(vmem_limit_bytes=62 * 2**20),
-    )(
-        key_sum,
-        router_sum,
-        gain_sum,
-        factor,
-        key_other,
-        router_other,
-        gain_other,
-        key_state,
-        router_state,
-        gain_state,
-    )
+        scratch_shapes=[
+            pltpu.VMEM((2, width // LANES, rows, LANES), BF16),
+            pltpu.VMEM((2, experts * steps, LANES), BF16),
+            pltpu.VMEM((2 * gain // 128 + 8, 128), F32),
+            pltpu.VMEM((2 * gain // 128, 128), F32),
+            pltpu.SemaphoreType.DMA((steps,)),
+            pltpu.SemaphoreType.DMA((2,)),
+        ],
+        compiler_params=pltpu.CompilerParams(vmem_limit_bytes=46 * 2**20),
+    )(packed, small, key_state, router_state, gain_state)
 
 
 def reduce_grads(
@@ -564,26 +592,18 @@
     plans = stage_shapes(total_rows // PARTS, wide_bits)
     stages = len(plans[0])
     count = math.prod(key_shape) + math.prod(router_shape) + gain_size
-    vmem = pl.BlockSpec(memory_space=pltpu.VMEM)
     hbm = pl.BlockSpec(memory_space=pl.ANY)
     half_rows, width = key_shape[0] // 2, key_shape[1]
-    experts, half_cols = router_shape[0], router_shape[1] // 2
-    pieces = half_rows // 4 // KEY_PIECE + 1
     return pl.pallas_call(
         functools.partial(
             reduce_kernel, plans, blocks, total_rows, 0.5 * math.sqrt(count)
         ),
         out_shape=(
-            jax.ShapeDtypeStruct((key_shape[0] // 2, key_shape[1]), BF16),
-            jax.ShapeDtypeStruct((router_shape[0], router_shape[1] // 2), BF16),
-            jax.ShapeDtypeStruct((1, gain_size // 2), F32),
-            jax.ShapeDtypeStruct((1, 128), F32),
-            jax.ShapeDtypeStruct((half_rows, width), BF16),
-            jax.ShapeDtypeStruct((experts, half_cols), BF16),
-            jax.ShapeDtypeStruct((1, gain_size // 2), F32),
+            jax.ShapeDtypeStruct((2, 4 * (width // LANES), half_rows, LANES), BF16),
+            jax.ShapeDtypeStruct((16 * half_rows, 128), F32),
         ),
         in_specs=[hbm] * 3 + [[hbm] * 3] * 3,
-        out_specs=(hbm, hbm, vmem, vmem, hbm, hbm, vmem),
+        out_specs=(hbm, hbm),
         scratch_shapes=[
             pltpu.VMEM((2, 2, total_rows, LANES), BF16),
             pltpu.VMEM((2, gain_size), BF16),
@@ -604,21 +624,20 @@
             pltpu.SemaphoreType.DMA((stages,)),
             pltpu.SemaphoreType.DMA((6,)),
             pltpu.SemaphoreType.DMA((6,)),
-            pltpu.VMEM((3, half_rows // 4, width), F32),
-            pltpu.VMEM((3, experts // 4, half_cols), F32),
+            pltpu.VMEM((3, total_rows, LANES), F32),
             pltpu.VMEM((3, 1, gain_size // 2), F32),
-            pltpu.VMEM((half_rows // 4, width), BF16),
-            pltpu.VMEM((experts // 4, half_cols), BF16),
-            pltpu.VMEM((half_rows, width), BF16),
-            pltpu.VMEM((experts, half_cols), BF16),
+            pltpu.VMEM((PARTS, total_rows // PARTS // 4, LANES), BF16),
+            pltpu.VMEM((total_rows, LANES), BF16),
             pltpu.VMEM((1, gain_size // 2), F32),
             pltpu.VMEM((1, gain_size // 2), F32),
+            pltpu.VMEM((1, gain_size // 2), F32),
+            pltpu.VMEM((gain_size // 128 + 8, 128), F32),
             pltpu.SemaphoreType.DMA((2 * (len(blocks) + PARTS) + 1,)),
-            pltpu.SemaphoreType.DMA((9,)),
-            pltpu.SemaphoreType.DMA((4, pieces)),
-            pltpu.SemaphoreType.DMA((4, pieces)),
+            pltpu.SemaphoreType.DMA((3 * (len(blocks) + 1),)),
+            pltpu.SemaphoreType.DMA((4, PARTS)),
+            pltpu.SemaphoreType.DMA((4, PARTS)),
             pltpu.SemaphoreType.DMA((2,)),
-            pltpu.SemaphoreType.DMA((len(blocks) + 2,)),
+            pltpu.SemaphoreType.DMA((2 * (width // LANES + 1) + 1,)),
         ],
         compiler_params=pltpu.CompilerParams(
             collective_id=0, has_side_effects=True, vmem_limit_bytes=56 * 2**20
@@ -648,7 +667,7 @@
         wide_size, key_grads, router_grads, gain_grads, key_state, router_state, gain_state
     )
     key_new, router_new, gain_new, key_weight, router_weight, gain_weight = update_all(
-        sums, key_state, router_state, gain_state
+        *sums, key_state, router_state, gain_state
     )
     return (
         *key_new,

time: 64.3 us -> 57.2 us (0.89)
  Pallas kernels: 62.1 us -> 55.9 us
  other arithmetic: 1.32 us -> 0 us
    pallas_call x1, Pallas kernels: 52.5 us -> 48.9 us  [reduce_grads(): pl.pallas_call(functools.partial(reduce_kernel, plans, blocks, total_rows...]
    pallas_call x1, Pallas kernels: 9.57 us -> 6.97 us  [update_all(): pl.pallas_call(update_kernel, grid=(steps,), out_shape=([shape((rows, wid...]
    pallas_call x1 -> x0, other arithmetic: 1.32 us -> none  [update_all(): pl.pallas_call(update_kernel, grid=(steps,), out_shape=([shape((rows, wid...]
where the time goes in v4:
time: 57.2 us; the launch traced here: 56.7 us
  Pallas kernels  55.9 us (98%)
  between operations  0.8 us (1%)
    pallas_call x1, Pallas kernels, reduce_grads(): pl.pallas_call(functools.partial(reduce_kernel, plans, blocks, total_rows...  48.9 us
    pallas_call x1, Pallas kernels, update_all(): pl.pallas_call(update_kernel, grid=(steps,), out_shape=([shape((rows, wid...  6.97 us

profile of v4, /device:TPU:0, one launch (start us, length us, event | category | flops | bytes accessed | tf_op | source)
XLA Modules:
  0.0 56.7 jit_solution(9108684543032592960)
XLA Ops:
  0.6 0.0 copy-start
  0.7 0.0 copy-start.1
  0.7 0.0 copy-start.2
  0.7 0.0 copy-start.3
  0.7 0.0 copy-start.4
  0.7 0.0 copy-start.5
  0.7 0.0 copy-start.6
  0.7 0.0 copy-start.7
  0.7 0.0 copy-start.8
  0.7 48.9 %shard_map.211 = (bf16[2,16,1024,128]{3,2,1,0:T(8,128)(2,1)}, f32[16384,128]{1,0:T(8,128)}) custom-call(bf16[1,1,2,2048,512]{4,3,2,1,0:T(8,128)(2,1)} %key_ref.1, bf16[1,1,2,64,2048]{4,3,2,1,0:T(8,128)(2,1)} %router_ref.1, bf16[1,1,2,2048]{3,2,1,0:T(2,128)(2,1)} %gain_ref.1, f32[1024,512]{1,0:T(8,128)} %key_state_0_.3, f32[1024,512]{1,0:T(8,128)} %key_state_1_.3, ...), custom_call_target="tpu_custom_call" | custom-call | tf_op jit(solution)/shard_map/pallas_call | solution.py:597
  49.7 0.0 copy-done
  49.7 0.0 copy-done.1
  49.7 0.0 copy-done.2
  49.7 0.0 copy-done.3
  49.7 0.0 copy-done.4
  49.7 0.0 copy-done.5
  49.7 0.0 copy-done.6
  49.7 0.0 copy-done.7
  49.8 0.0 copy-done.8
  49.8 7.0 %shard_map.212 = (f32[1024,512]{1,0:T(8,128)}, f32[1024,512]{1,0:T(8,128)}, f32[1024,512]{1,0:T(8,128)}, f32[64,1024]{1,0:T(8,128)}, f32[64,1024]{1,0:T(8,128)},...) custom-call(bf16[2,16,1024,128]{3,2,1,0:T(8,128)(2,1)} %get-tuple-el, ...), custom_call_target="tpu_custom_call" | custom-call | tf_op jit(solution)/shard_map/pallas_call | solution.py:552
Async XLA Ops:
  0.6 49.0 %copy-start = (f32[1024,512]{1,0:T(8,128)S(1)}, f32[1024,512]{1,0:T(8,128)}, u32[]{:S(2)}) copy-start(f32[1024,512]{1,0:T(8,128)} %key_state_0_.3) | copy-start | bytes 6291460
  0.7 49.0 %copy-start.1 = (f32[1024,512]{1,0:T(8,128)S(1)}, f32[1024,512]{1,0:T(8,128)}, u32[]{:S(2)}) copy-start(f32[1024,512]{1,0:T(8,128)} %key_state_1_.3) | copy-start | bytes 6291460
  0.7 49.0 %copy-start.2 = (f32[1024,512]{1,0:T(8,128)S(1)}, f32[1024,512]{1,0:T(8,128)}, u32[]{:S(2)}) copy-start(f32[1024,512]{1,0:T(8,128)} %key_state_2_.3) | copy-start | bytes 6291460
  0.7 49.0 %copy-start.3 = (f32[64,1024]{1,0:T(8,128)S(1)}, f32[64,1024]{1,0:T(8,128)}, u32[]{:S(2)}) copy-start(f32[64,1024]{1,0:T(8,128)} %router_state_0_.3) | copy-start | bytes 786436
  0.7 49.0 %copy-start.4 = (f32[64,1024]{1,0:T(8,128)S(1)}, f32[64,1024]{1,0:T(8,128)}, u32[]{:S(2)}) copy-start(f32[64,1024]{1,0:T(8,128)} %router_state_1_.3) | copy-start | bytes 786436
  0.7 49.0 %copy-start.5 = (f32[64,1024]{1,0:T(8,128)S(1)}, f32[64,1024]{1,0:T(8,128)}, u32[]{:S(2)}) copy-start(f32[64,1024]{1,0:T(8,128)} %router_state_2_.3) | copy-start | bytes 786436
  0.7 49.0 %copy-start.6 = (f32[1024]{0:T(1024)S(1)}, f32[1024]{0:T(1024)}, u32[]{:S(2)}) copy-start(f32[1024]{0:T(1024)} %param.21) | copy-start | bytes 12292
  0.7 49.0 %copy-start.7 = (f32[1024]{0:T(1024)S(1)}, f32[1024]{0:T(1024)}, u32[]{:S(2)}) copy-start(f32[1024]{0:T(1024)} %param.22) | copy-start | bytes 12292
  0.7 49.0 %copy-start.8 = (f32[1024]{0:T(1024)S(1)}, f32[1024]{0:T(1024)}, u32[]{:S(2)}) copy-start(f32[1024]{0:T(1024)} %param.23) | copy-start | bytes 12292

commit v5 on v4

--- a/solution.py
+++ b/solution.py
@@ -25,7 +25,8 @@
     scaled = factor * gradient
     first_new = beta_one * first_moment + (1.0 - beta_one) * scaled
     second_new = beta_two * second + (1.0 - beta_two) * scaled * scaled
-    root = jnp.sqrt(second_new * (1.0 / bias_two)) + epsilon
+    spread = second_new * (1.0 / bias_two)
+    root = spread * lax.rsqrt(spread) + epsilon
     update = first_new * (1.0 / bias_one) / root
     if decay_rate:
         update = update + decay_rate * master
@@ -221,27 +222,27 @@
         copy.start()
         state_loads.append(copy)
 
-    for i in range(3):
-        load_state(gain_state[i], gain_mine.at[i])
-        for at, count, kind, col in blocks:
-            source = key_state[i] if kind == "key" else router_state[i]
-            load_state(source.at[:, pl.ds(col, LANES)], state.at[i, pl.ds(at, count), :])
-
     base = [pl.multiple_of(p * part_rows + bit[0] * (part_rows // 2), 16) for p in range(PARTS)]
     rows_now = [part_rows // 2] * PARTS
     split = [False] * PARTS
 
-    def add(p, stage, half, h, offset, r, step):
+    def add(p, stage, half, h, start, offset, r, step):
         previous = local if stage == 0 else acc
-        mine = previous[half, pl.ds(pl.multiple_of(base[p] + offset + r, 16), step), :]
+        mine = previous[half, pl.ds(pl.multiple_of(start + offset + r, 16), step), :]
         theirs = recv_bufs[p][stage][h, pl.ds(pl.multiple_of(offset + r, 16), step), :]
         return mine.astype(F32) + theirs.astype(F32)
 
     for stage in range(1, stages):
+        if stage == 2:
+            for i in range(3):
+                load_state(gain_state[i], gain_mine.at[i])
+                for at, count, kind, col in blocks:
+                    source = key_state[i] if kind == "key" else router_state[i]
+                    load_state(source.at[:, pl.ds(col, LANES)], state.at[i, pl.ds(at, count), :])
         gain_copies[stage - 1].wait_recv()
         gain_val[stage] = gain_val[stage - 1] + gain_in[stage - 1]
         send_gain(stage)
-        fresh = []
+        fresh, pending = [], []
         for p in range(PARTS):
             axis, shape = plans[p][stage]
             copies[p].wait_recv()
@@ -262,7 +263,7 @@
 
             def out(r, p=p):
                 for half, h, slot in send_sets:
-                    value = add(p, stage - 1, half, h, send_offset, r, step)
+                    value = add(p, stage - 1, half, h, base[p], send_offset, r, step)
                     send_buf[slot, pl.ds(r, step), :] = value.astype(BF16)
                     if not keep_sets:
                         rows = pl.ds(pl.multiple_of(base[p] + r, 16), step)
@@ -280,18 +281,24 @@
             fresh.append(copy)
             started.append(copy)
 
-            def keep(r, p=p):
-                for half, h in keep_sets:
-                    value = add(p, stage - 1, half, h, keep_offset, r, step)
-                    rows = pl.ds(pl.multiple_of(base[p] + keep_offset + r, 16), step)
+            def keep(
+                r, p=p, sets=keep_sets, start=base[p], offset=keep_offset, step=step
+            ):
+                for half, h in sets:
+                    value = add(p, stage - 1, half, h, start, offset, r, step)
+                    rows = pl.ds(pl.multiple_of(start + offset + r, 16), step)
                     acc[half, rows, :] = value
 
             if keep_sets:
-                rows_loop(shape[1], step, keep)
+                pending.append((shape[1], step, keep))
             if axis == "x":
                 split[p] = True
             base[p] = pl.multiple_of(base[p] + keep_offset, 16)
             rows_now[p] = shape[1]
+            if p % 3 == 2:
+                for job in pending:
+                    rows_loop(*job)
+                pending = []
         copies = fresh
 
     gather_axes = [
@@ -319,7 +326,7 @@
     for p in range(PARTS):
         copies[p].wait_recv()
         count = rows_now[p]
-        value = add(p, stages - 1, narrow, 0, 0, 0, count)
+        value = add(p, stages - 1, narrow, 0, base[p], 0, 0, count)
         full[pl.ds(base[p], count), :] = value.astype(BF16)
         gathers.append(gather(p, 0))
         squares = squares + jnp.sum((value * value).reshape(count // 8, 8, LANES), axis=0)

time: 57.2 us -> 56.7 us (level)
  no operation moved by 1% of the time
where the time goes in v5:
time: 56.7 us; the launch traced here: 56.4 us
  Pallas kernels  55.6 us (98%)
  between operations  0.8 us (1%)
    pallas_call x1, Pallas kernels, reduce_grads(): pl.pallas_call(functools.partial(reduce_kernel, plans, blocks, total_rows...  48.8 us
    pallas_call x1, Pallas kernels, update_all(): pl.pallas_call(update_kernel, grid=(steps,), out_shape=([shape((rows, wid...  6.73 us

profile of v5, /device:TPU:0, one launch (start us, length us, event | category | flops | bytes accessed | tf_op | source)
XLA Modules:
  0.0 56.4 jit_solution(2602380775146391623)
XLA Ops:
  0.6 0.0 copy-start
  0.7 0.0 copy-start.1
  0.7 0.0 copy-start.2
  0.7 0.0 copy-start.3
  0.7 0.0 copy-start.4
  0.7 0.0 copy-start.5
  0.7 0.0 copy-start.6
  0.7 0.0 copy-start.7
  0.7 0.0 copy-start.8
  0.7 48.8 %shard_map.211 = (bf16[2,16,1024,128]{3,2,1,0:T(8,128)(2,1)}, f32[16384,128]{1,0:T(8,128)}) custom-call(bf16[1,1,2,2048,512]{4,3,2,1,0:T(8,128)(2,1)} %key_ref.1, bf16[1,1,2,64,2048]{4,3,2,1,0:T(8,128)(2,1)} %router_ref.1, bf16[1,1,2,2048]{3,2,1,0:T(2,128)(2,1)} %gain_ref.1, f32[1024,512]{1,0:T(8,128)} %key_state_0_.3, f32[1024,512]{1,0:T(8,128)} %key_state_1_.3, ...), custom_call_target="tpu_custom_call" | custom-call | tf_op jit(solution)/shard_map/pallas_call | solution.py:604
  49.6 0.0 copy-done
  49.6 0.0 copy-done.1
  49.6 0.0 copy-done.2
  49.6 0.0 copy-done.3
  49.6 0.0 copy-done.4
  49.6 0.0 copy-done.5
  49.6 0.0 copy-done.6
  49.7 0.0 copy-done.7
  49.7 0.0 copy-done.8
  49.7 6.7 %shard_map.212 = (f32[1024,512]{1,0:T(8,128)}, f32[1024,512]{1,0:T(8,128)}, f32[1024,512]{1,0:T(8,128)}, f32[64,1024]{1,0:T(8,128)}, f32[64,1024]{1,0:T(8,128)},...) custom-call(bf16[2,16,1024,128]{3,2,1,0:T(8,128)(2,1)} %get-tuple-el, ...), custom_call_target="tpu_custom_call" | custom-call | tf_op jit(solution)/shard_map/pallas_call | solution.py:559
Async XLA Ops:
  0.6 48.9 %copy-start = (f32[1024,512]{1,0:T(8,128)S(1)}, f32[1024,512]{1,0:T(8,128)}, u32[]{:S(2)}) copy-start(f32[1024,512]{1,0:T(8,128)} %key_state_0_.3) | copy-start | bytes 6291460
  0.7 48.9 %copy-start.1 = (f32[1024,512]{1,0:T(8,128)S(1)}, f32[1024,512]{1,0:T(8,128)}, u32[]{:S(2)}) copy-start(f32[1024,512]{1,0:T(8,128)} %key_state_1_.3) | copy-start | bytes 6291460
  0.7 48.9 %copy-start.2 = (f32[1024,512]{1,0:T(8,128)S(1)}, f32[1024,512]{1,0:T(8,128)}, u32[]{:S(2)}) copy-start(f32[1024,512]{1,0:T(8,128)} %key_state_2_.3) | copy-start | bytes 6291460
  0.7 48.9 %copy-start.3 = (f32[64,1024]{1,0:T(8,128)S(1)}, f32[64,1024]{1,0:T(8,128)}, u32[]{:S(2)}) copy-start(f32[64,1024]{1,0:T(8,128)} %router_state_0_.3) | copy-start | bytes 786436
  0.7 48.9 %copy-start.4 = (f32[64,1024]{1,0:T(8,128)S(1)}, f32[64,1024]{1,0:T(8,128)}, u32[]{:S(2)}) copy-start(f32[64,1024]{1,0:T(8,128)} %router_state_1_.3) | copy-start | bytes 786436
  0.7 48.9 %copy-start.5 = (f32[64,1024]{1,0:T(8,128)S(1)}, f32[64,1024]{1,0:T(8,128)}, u32[]{:S(2)}) copy-start(f32[64,1024]{1,0:T(8,128)} %router_state_2_.3) | copy-start | bytes 786436
  0.7 48.9 %copy-start.6 = (f32[1024]{0:T(1024)S(1)}, f32[1024]{0:T(1024)}, u32[]{:S(2)}) copy-start(f32[1024]{0:T(1024)} %param.21) | copy-start | bytes 12292
  0.7 48.9 %copy-start.7 = (f32[1024]{0:T(1024)S(1)}, f32[1024]{0:T(1024)}, u32[]{:S(2)}) copy-start(f32[1024]{0:T(1024)} %param.22) | copy-start | bytes 12292
  0.7 48.9 %copy-start.8 = (f32[1024]{0:T(1024)S(1)}, f32[1024]{0:T(1024)}, u32[]{:S(2)}) copy-start(f32[1024]{0:T(1024)} %param.23) | copy-start | bytes 12292

commit v6 on v5

--- a/solution.py
+++ b/solution.py
@@ -54,7 +54,10 @@
 
 
 def part_orders():
-    return (("x", 1, 2), (1, 2, "x"), (2, "x", 1)) * (PARTS // 3)
+    return (
+        ("x", 1, 2), (1, 2, "x"), (2, "x", 1),
+        ("x", 2, 1), (1, "x", 2), (2, 1, "x"),
+    )
 
 
 def stage_shapes(part_rows, wide_bits):

time: 56.7 us -> 57.2 us (level)
  no operation moved by 1% of the time
where the time goes in v6:
time: 57.2 us; the launch traced here: 56.8 us
  Pallas kernels  56 us (98%)
  between operations  0.8 us (1%)
    pallas_call x1, Pallas kernels, reduce_grads(): pl.pallas_call(functools.partial(reduce_kernel, plans, blocks, total_rows...  49.3 us
    pallas_call x1, Pallas kernels, update_all(): pl.pallas_call(update_kernel, grid=(steps,), out_shape=([shape((rows, wid...  6.73 us

profile of v6, /device:TPU:0, one launch (start us, length us, event | category | flops | bytes accessed | tf_op | source)
XLA Modules:
  0.0 56.8 jit_solution(10444340307294345339)
XLA Ops:
  0.6 0.0 copy-start
  0.7 0.0 copy-start.1
  0.7 0.0 copy-start.2
  0.7 0.0 copy-start.3
  0.7 0.0 copy-start.4
  0.7 0.0 copy-start.5
  0.7 0.0 copy-start.6
  0.7 0.0 copy-start.7
  0.7 0.0 copy-start.8
  0.7 49.3 %shard_map.211 = (bf16[2,16,1024,128]{3,2,1,0:T(8,128)(2,1)}, f32[16384,128]{1,0:T(8,128)}) custom-call(bf16[1,1,2,2048,512]{4,3,2,1,0:T(8,128)(2,1)} %key_ref.1, bf16[1,1,2,64,2048]{4,3,2,1,0:T(8,128)(2,1)} %router_ref.1, bf16[1,1,2,2048]{3,2,1,0:T(2,128)(2,1)} %gain_ref.1, f32[1024,512]{1,0:T(8,128)} %key_state_0_.3, f32[1024,512]{1,0:T(8,128)} %key_state_1_.3, ...), custom_call_target="tpu_custom_call" | custom-call | tf_op jit(solution)/shard_map/pallas_call | solution.py:607
  50.0 0.0 copy-done
  50.0 0.0 copy-done.1
  50.0 0.0 copy-done.2
  50.1 0.0 copy-done.3
  50.1 0.0 copy-done.4
  50.1 0.0 copy-done.5
  50.1 0.0 copy-done.6
  50.1 0.0 copy-done.7
  50.1 0.0 copy-done.8
  50.1 6.7 %shard_map.212 = (f32[1024,512]{1,0:T(8,128)}, f32[1024,512]{1,0:T(8,128)}, f32[1024,512]{1,0:T(8,128)}, f32[64,1024]{1,0:T(8,128)}, f32[64,1024]{1,0:T(8,128)},...) custom-call(bf16[2,16,1024,128]{3,2,1,0:T(8,128)(2,1)} %get-tuple-el, ...), custom_call_target="tpu_custom_call" | custom-call | tf_op jit(solution)/shard_map/pallas_call | solution.py:562
Async XLA Ops:
  0.6 49.4 %copy-start = (f32[1024,512]{1,0:T(8,128)S(1)}, f32[1024,512]{1,0:T(8,128)}, u32[]{:S(2)}) copy-start(f32[1024,512]{1,0:T(8,128)} %key_state_0_.3) | copy-start | bytes 6291460
  0.7 49.4 %copy-start.1 = (f32[1024,512]{1,0:T(8,128)S(1)}, f32[1024,512]{1,0:T(8,128)}, u32[]{:S(2)}) copy-start(f32[1024,512]{1,0:T(8,128)} %key_state_1_.3) | copy-start | bytes 6291460
  0.7 49.4 %copy-start.2 = (f32[1024,512]{1,0:T(8,128)S(1)}, f32[1024,512]{1,0:T(8,128)}, u32[]{:S(2)}) copy-start(f32[1024,512]{1,0:T(8,128)} %key_state_2_.3) | copy-start | bytes 6291460
  0.7 49.4 %copy-start.3 = (f32[64,1024]{1,0:T(8,128)S(1)}, f32[64,1024]{1,0:T(8,128)}, u32[]{:S(2)}) copy-start(f32[64,1024]{1,0:T(8,128)} %router_state_0_.3) | copy-start | bytes 786436
  0.7 49.4 %copy-start.4 = (f32[64,1024]{1,0:T(8,128)S(1)}, f32[64,1024]{1,0:T(8,128)}, u32[]{:S(2)}) copy-start(f32[64,1024]{1,0:T(8,128)} %router_state_1_.3) | copy-start | bytes 786436
  0.7 49.4 %copy-start.5 = (f32[64,1024]{1,0:T(8,128)S(1)}, f32[64,1024]{1,0:T(8,128)}, u32[]{:S(2)}) copy-start(f32[64,1024]{1,0:T(8,128)} %router_state_2_.3) | copy-start | bytes 786436
  0.7 49.4 %copy-start.6 = (f32[1024]{0:T(1024)S(1)}, f32[1024]{0:T(1024)}, u32[]{:S(2)}) copy-start(f32[1024]{0:T(1024)} %param.21) | copy-start | bytes 12292
  0.7 49.4 %copy-start.7 = (f32[1024]{0:T(1024)S(1)}, f32[1024]{0:T(1024)}, u32[]{:S(2)}) copy-start(f32[1024]{0:T(1024)} %param.22) | copy-start | bytes 12292
  0.7 49.4 %copy-start.8 = (f32[1024]{0:T(1024)S(1)}, f32[1024]{0:T(1024)}, u32[]{:S(2)}) copy-start(f32[1024]{0:T(1024)} %param.23) | copy-start | bytes 12292
